TPU v7x, 256 devices: a whole 4x4x8 slice. The times are simulated.
256 devices in a mesh: dp: 8 (over z), expert: 8 (over y, core), tensor: 4 (over x).
Axes of the slice: x: 4, y: 4, z: 8, core: 2. Of those that a mesh axis runs over, the one named last changes fastest.
Arguments:
- tokens: bfloat16 [1024, 6144], P('dp', 'expert'), may hold values from -6 to 6
- out_grad: bfloat16 [1024, 6144], P('dp', 'expert'), may hold values from -3 to 3
- expert_ids: int32 [1024, 2], P('dp'), may hold values from 0 to 7, all different within a row; in each aligned block of 128 rows (0 to 127, 128 to 255, ...) at most 48 rows name the same one
- combine_weights: float32 [1024, 2], P('dp'), may hold values from 0.05 to 1
- w_gate: bfloat16 [8, 6144, 8192], P('expert', None, ('dp', 'tensor')), may hold values from -0.078125 to 0.078125
- w_up: bfloat16 [8, 6144, 8192], P('expert', None, ('dp', 'tensor')), may hold values from -0.078125 to 0.078125
- w_down: bfloat16 [8, 8192, 6144], P('expert', ('dp', 'tensor')), may hold values from -0.0625 to 0.0625
Outputs:
- x_grad: bfloat16 [1024, 6144], P('dp', 'expert')
- router_grad: float32 [1024, 2], P('dp')
Inputs may be any that keep to these rules, and one draw needn't show every extreme that they name: `expert_ids`: in each aligned block of 128 tokens (the tokens of one index of dp) at most 48 entries name one expert, a bound that the crowded blocks reach; the two experts of a token differ.
All inputs are finite; a program needn't handle non-finite values.
Results may differ from a plain program's by a relative error of at most 0.0049.
Values may be sent and summed in bfloat16 or wider, within the bound.
No kernel may reach another device: no remote copies, remote signals or barrier semaphores. Data moves between devices by JAX's collectives and lax.ppermute only.
A program may use at most 128 MiB of HBM per device.

v0:
```python
import functools

import jax
import jax.numpy as jnp
from jax import lax
from jax.experimental import pallas as pl
from jax.experimental.pallas import tpu as pltpu
from jax.sharding import PartitionSpec as P

EXPERTS = 8
CAP = 48
WHOLE = 256
PART = 128
AHEAD = 4
BF = jnp.bfloat16
F32 = jnp.float32
HIGH = lax.Precision.HIGHEST


def nt(a, b, **kw):
    return lax.dot_general(a, b, (((1,), (1,)), ((), ())), preferred_element_type=F32, **kw)


def tn(a, b, **kw):
    return lax.dot_general(a, b, (((0,), (0,)), ((), ())), preferred_element_type=F32, **kw)


def slot_masks(ids):
    tokens = ids.shape[1]
    experts = lax.broadcasted_iota(jnp.int32, (EXPERTS, tokens), 0)
    ind0 = (ids[0:1, :] == experts).astype(F32)
    ind1 = (ids[1:2, :] == experts).astype(F32)
    before = (
        lax.broadcasted_iota(jnp.int32, (tokens, tokens), 0)
        < lax.broadcasted_iota(jnp.int32, (tokens, tokens), 1)
    )
    count = jnp.dot((ind0 + ind1).astype(BF), before.astype(BF), preferred_element_type=F32)
    return ind0, ind1, count.astype(jnp.int32)


def dispatch_kernel(place_ref, ids_ref, tok_ref, og_ref, out_ref):
    ind0, ind1, count = slot_masks(ids_ref[...])
    ind = ind0 + ind1
    tokens = ind.shape[1]
    slots = lax.broadcasted_iota(jnp.int32, (CAP, tokens), 0)
    quarter = pl.ds(pl.multiple_of(WHOLE + place_ref[0] * PART, 128), PART)
    og = jnp.concatenate([og_ref[:, 0:WHOLE], og_ref[:, quarter]], axis=1)
    for e in range(EXPERTS):
        pick = jnp.where(count[e : e + 1, :] == slots, ind[e : e + 1, :], 0.0).astype(BF)
        width = tok_ref.shape[1]
        out_ref[e, :, :width] = jnp.dot(
            pick, tok_ref[...], preferred_element_type=F32
        ).astype(BF)
        out_ref[e, :, width:] = jnp.dot(pick, og, preferred_element_type=F32).astype(BF)


def dispatch(place, ids, tokens, out_grad):
    width = tokens.shape[1]
    return pl.pallas_call(
        dispatch_kernel,
        in_specs=[pl.BlockSpec(memory_space=pltpu.SMEM)]
        + [pl.BlockSpec(memory_space=pltpu.VMEM)] * 3,
        out_shape=jax.ShapeDtypeStruct((EXPERTS, CAP, width + WHOLE + PART), BF),
        compiler_params=pltpu.CompilerParams(vmem_limit_bytes=24 << 20),
        name="dispatch",
    )(place, ids, tokens, out_grad)


def forward_kernel(count, split, n_after, place_ref, *refs):
    toks, ogs = refs[: count + split], refs[count + split : 2 * (count + split)]
    refs = refs[2 * (count + split) :]
    owns = refs[:count]
    quarters = [refs[count + 3 * i : count + 3 * i + 3] for i in range(count)]
    refs = refs[4 * count + n_after :]
    wg_ref, wu_ref, wd_ref = refs[:3]
    outs = refs[3 : 3 + 2 * count]
    acc_g, acc_u, acc_b, og_ref = refs[3 + 2 * count :]
    e = pl.program_id(0)

    @pl.when(e == 0)
    def _():
        acc_g[...] = jnp.zeros_like(acc_g)
        acc_u[...] = jnp.zeros_like(acc_u)
        acc_b[...] = jnp.zeros_like(acc_b)

    tok, og = [r[0] for r in toks[:count]], [r[0] for r in ogs[:count]]
    if split:
        tok[-1] = jnp.where(e < AHEAD, tok[-1], toks[count][0])
        og[-1] = jnp.where(e < AHEAD, og[-1], ogs[count][0])
    tok = jnp.concatenate(tok, axis=0)
    for i in range(count):
        rows = slice(i * CAP, (i + 1) * CAP)
        og_ref[rows, 0:WHOLE] = og[i]
        pieces = [owns[i][0], *[r[0, 0] for r in quarters[i]]]
        for piece, offset in zip(pieces, (0, 3, 1, 2)):
            there = lax.rem(place_ref[0] + offset, 4)
            og_ref[rows, pl.ds(pl.multiple_of(WHOLE + there * PART, 128), PART)] = piece
    acc_g[...] += jnp.dot(tok, wg_ref[0], preferred_element_type=F32)
    acc_u[...] += jnp.dot(tok, wu_ref[0], preferred_element_type=F32)
    acc_b[...] += nt(og_ref[...], wd_ref[0])

    @pl.when(e == EXPERTS - 1)
    def _():
        gate, up, back = acc_g[...], acc_u[...], acc_b[...]
        sig = jax.nn.sigmoid(gate)
        act = gate * sig
        prod = back * (act * up)
        grad_up = (back * act).astype(BF)
        grad_gate = (back * up * sig * (1.0 + gate * (1.0 - sig))).astype(BF)
        hidden = gate.shape[1]
        ones = jnp.ones((16, hidden), F32)
        fill = jnp.zeros((128 - CAP, hidden), F32)
        for i in range(count):
            rows = slice(i * CAP, (i + 1) * CAP)
            outs[2 * i][:, :hidden] = grad_gate[rows]
            outs[2 * i][:, hidden:] = grad_up[rows]
            outs[2 * i + 1][...] = nt(
                ones, jnp.concatenate([prod[rows], fill], axis=0), precision=HIGH
            )


def forward(place, blocks, owns, quarters, after, w_gate, w_up, w_down):
    hidden = w_gate.shape[2]
    width = w_gate.shape[1] // EXPERTS
    count = len(quarters)
    split = len(blocks) - count
    slices = [lambda e: e] * count
    if split:
        slices[-1:] = [
            lambda e: jnp.minimum(e, AHEAD - 1),
            lambda e: jnp.maximum(e - AHEAD, 0),
        ]

    def tok_spec(at):
        return pl.BlockSpec((1, CAP, width), lambda e, _: (at(e), 0, 0))

    def og_spec(at):
        return pl.BlockSpec((1, CAP, WHOLE), lambda e, _: (at(e), 0, width // WHOLE))

    def own_spec(column):
        return pl.BlockSpec((1, CAP, PART), lambda e, _: (e, 0, column))

    in_specs = [tok_spec(at) for at in slices] + [og_spec(at) for at in slices]
    in_specs += [own_spec(a.shape[2] // PART - 1) for a in owns]
    operands = []

    def quarter_spec(index):
        return pl.BlockSpec((1, 1, CAP, PART), lambda e, at: (index, e, 0, 0))

    for index, arrays in quarters:
        in_specs += [quarter_spec(index)] * 3
        operands += arrays
    in_specs += [pl.BlockSpec(memory_space=pl.ANY)] * len(after)
    in_specs += [
        pl.BlockSpec((1, width, hidden), lambda e, at: (0, e, 0)),
        pl.BlockSpec((1, width, hidden), lambda e, at: (0, e, 0)),
        pl.BlockSpec((1, hidden, width), lambda e, at: (0, 0, e)),
    ]
    rows = count * CAP
    outs = pl.pallas_call(
        functools.partial(forward_kernel, count, split, len(after)),
        grid_spec=pltpu.PrefetchScalarGridSpec(
            num_scalar_prefetch=1,
            grid=(EXPERTS,),
            in_specs=in_specs,
            out_specs=[
                pl.BlockSpec((CAP, 2 * hidden), lambda e, at: (0, 0)),
                pl.BlockSpec((16, 128), lambda e, at: (0, 0)),
            ]
            * count,
            scratch_shapes=[pltpu.VMEM((rows, hidden), F32)] * 3 + [pltpu.VMEM((rows, width), BF)],
        ),
        out_shape=[
            jax.ShapeDtypeStruct((CAP, 2 * hidden), BF),
            jax.ShapeDtypeStruct((16, 128), F32),
        ]
        * count,
        compiler_params=pltpu.CompilerParams(vmem_limit_bytes=24 << 20),
        cost_estimate=pl.CostEstimate(
            flops=6 * 256 * EXPERTS * width * hidden,
            bytes_accessed=6 * EXPERTS * width * hidden,
            transcendentals=0,
        ),
        name="forward",
    )(place, *blocks, *blocks, *owns, *operands, *after, w_gate, w_up, w_down)
    return [(outs[2 * i], outs[2 * i + 1]) for i in range(count)]


def pack_slots(total, width):
    high = total.astype(BF).astype(F32)
    low = total - high
    row = lax.broadcasted_iota(jnp.int32, (16, 128), 0)
    packed = jnp.where(row == 0, high, jnp.where(row == 1, low, 0.0)).astype(BF)
    return jnp.concatenate([packed, jnp.zeros((16, width - 128), BF)], axis=1)


def unpack_slots(rows):
    packed = rows.astype(F32)
    return packed[0:1] + packed[1:2]


def product(grads, wg_ref, wu_ref, e):
    hidden = wg_ref.shape[2]
    width = wg_ref.shape[1] // EXPERTS
    part = pl.ds(pl.multiple_of(e * width, width), width)
    return nt(grads[:, :hidden], wg_ref[0, part, :]) + nt(grads[:, hidden:], wu_ref[0, part, :])


def backward_kernel(ways, got, first, wg_ref, wu_ref, *refs):
    grads, slots, received, outs = (refs[i * ways : (i + 1) * ways] for i in range(4))
    if not got:
        outs = received
    skip = 0 if first else 16
    if not first:
        for i in range(ways):
            total = slots[i][0:1, :]
            if got:
                total = total + unpack_slots(received[i][0:16, 0:128])
            outs[i][0:16, :] = pack_slots(total, outs[i].shape[1])
    rows_of = jnp.concatenate([r[...] for r in grads], axis=0)

    @pl.loop(0, EXPERTS // 2)
    def _(e):
        part = product(rows_of, wg_ref, wu_ref, first + e)
        rows = pl.ds(pl.multiple_of(skip + e * CAP, 16), CAP)
        for i in range(ways):
            own = part[i * CAP : (i + 1) * CAP]
            if got:
                own = own + received[i][rows, :].astype(F32)
            outs[i][rows, :] = own.astype(BF)


def backward(first, small, received, w_gate, w_up):
    hidden = w_gate.shape[2]
    width = w_gate.shape[1] // EXPERTS
    ways = len(small)
    rows = CAP * EXPERTS // 2 + (0 if first else 16)
    operands = [w_gate, w_up, *[a for a, _ in small], *[a for _, a in small], *received]
    return pl.pallas_call(
        functools.partial(backward_kernel, ways, bool(received), first),
        in_specs=[pl.BlockSpec(memory_space=pltpu.VMEM)] * len(operands),
        out_shape=[jax.ShapeDtypeStruct((rows, width), BF)] * ways,
        compiler_params=pltpu.CompilerParams(vmem_limit_bytes=24 << 20),
        cost_estimate=pl.CostEstimate(
            flops=2 * 256 * EXPERTS * width * hidden,
            bytes_accessed=2 * EXPERTS * width * hidden,
            transcendentals=0,
        ),
        name="backward",
    )(*operands)


def own_kernel(g_ref, wg_ref, wu_ref, out_ref):
    grads = g_ref[...]

    @pl.loop(0, EXPERTS)
    def _(e):
        out_ref[e] = product(grads, wg_ref, wu_ref, e)


def own_product(grads, w_gate, w_up):
    hidden = w_gate.shape[2]
    width = w_gate.shape[1] // EXPERTS
    return pl.pallas_call(
        own_kernel,
        in_specs=[pl.BlockSpec(memory_space=pltpu.VMEM)] * 3,
        out_shape=jax.ShapeDtypeStruct((EXPERTS, CAP, width), F32),
        compiler_params=pltpu.CompilerParams(vmem_limit_bytes=24 << 20),
        cost_estimate=pl.CostEstimate(
            flops=2 * 256 * EXPERTS * width * hidden,
            bytes_accessed=4 * EXPERTS * width * hidden,
            transcendentals=0,
        ),
        name="own_product",
    )(grads, w_gate, w_up)


def last_kernel(own_ref, s_ref, *refs):
    low, high, out_ref = refs[0:2], refs[2:4], refs[4]
    half = EXPERTS // 2
    total = s_ref[0:1, :] + (unpack_slots(low[0][0:16, 0:128]) + unpack_slots(low[1][0:16, 0:128]))
    tail = pack_slots(total, out_ref.shape[2])
    for e in range(EXPERTS):
        parts, start = (low, 16 + e * CAP) if e < half else (high, (e - half) * CAP)
        rows = slice(start, start + CAP)
        sums = parts[0][rows, :].astype(F32) + parts[1][rows, :].astype(F32)
        out_ref[e, 0:CAP, :] = (own_ref[e] + sums).astype(BF)
        out_ref[e, CAP : CAP + 16, :] = tail


def last(own, slots, low, high):
    operands = [own, slots, *low, *high]
    return pl.pallas_call(
        last_kernel,
        in_specs=[pl.BlockSpec(memory_space=pltpu.VMEM)] * len(operands),
        out_shape=jax.ShapeDtypeStruct((EXPERTS, CAP + 16, own.shape[2]), BF),
        compiler_params=pltpu.CompilerParams(vmem_limit_bytes=24 << 20),
        name="last",
    )(*operands)


def combine_kernel(ids_ref, weight_ref, rows_ref, out_ref):
    ind0, ind1, count = slot_masks(ids_ref[...])
    tokens = ind0.shape[1]
    width = rows_ref.shape[2]
    weights = weight_ref[...]
    scale = ind0 * weights[0:1, :] + ind1 * weights[1:2, :]
    slots = lax.broadcasted_iota(jnp.int32, (CAP, tokens), 0)
    picks = []
    router0 = jnp.zeros((16, tokens), F32)
    router1 = jnp.zeros((16, tokens), F32)
    for e in range(EXPERTS):
        here = count[e : e + 1, :] == slots
        picks.append(jnp.where(here, scale[e : e + 1, :], 0.0))
        slot_rows = rows_ref[e, CAP : CAP + 16, 0:128][:, :CAP]
        one0 = jnp.where(here, ind0[e : e + 1, :], 0.0).astype(BF)
        one1 = jnp.where(here, ind1[e : e + 1, :], 0.0).astype(BF)
        router0 += jnp.dot(slot_rows, one0, preferred_element_type=F32)
        router1 += jnp.dot(slot_rows, one1, preferred_element_type=F32)
    rest = jnp.concatenate(picks, axis=0)
    rows = jnp.concatenate([rows_ref[e, 0:CAP, :] for e in range(EXPERTS)], axis=0)
    total = jnp.zeros((tokens, width), F32)
    for _ in range(3):
        part = rest.astype(BF)
        total += tn(part, rows)
        rest = rest - part.astype(F32)
    out_ref[0:tokens, :] = total.astype(BF)
    sum0 = router0[0:1] + router0[1:2]
    sum1 = router1[0:1] + router1[1:2]
    high0, high1 = sum0.astype(BF).astype(F32), sum1.astype(BF).astype(F32)
    row = lax.broadcasted_iota(jnp.int32, (16, tokens), 0)
    packed = jnp.where(row == 0, high0, 0.0) + jnp.where(row == 1, sum0 - high0, 0.0)
    packed = packed + jnp.where(row == 2, high1, 0.0) + jnp.where(row == 3, sum1 - high1, 0.0)
    out_ref[tokens : tokens + 16, :] = jnp.concatenate(
        [packed.astype(BF), jnp.zeros((16, width - tokens), BF)], axis=1
    )


def combine(ids, weights, rows):
    tokens = ids.shape[1]
    return pl.pallas_call(
        combine_kernel,
        out_shape=jax.ShapeDtypeStruct((tokens + 16, rows.shape[2]), BF),
        compiler_params=pltpu.CompilerParams(vmem_limit_bytes=24 << 20),
        name="combine",
    )(ids, weights, rows)


def finish_kernel(a_ref, b_ref, c_ref, d_ref, x_ref, r_ref):
    tokens = x_ref.shape[0]
    total = (a_ref[...].astype(F32) + c_ref[...].astype(F32)) + (
        b_ref[...].astype(F32) + d_ref[...].astype(F32)
    )
    x_ref[...] = total[:tokens].astype(BF)
    tail = total[tokens : tokens + 16, :tokens]
    r_ref[0:1, :] = tail[0:1] + tail[1:2]
    r_ref[1:2, :] = tail[2:3] + tail[3:4]


def finish(own, plus, two, minus):
    tokens = own.shape[0] - 16
    return pl.pallas_call(
        finish_kernel,
        out_shape=(
            jax.ShapeDtypeStruct((tokens, own.shape[1]), BF),
            jax.ShapeDtypeStruct((2, tokens), F32),
        ),
        compiler_params=pltpu.CompilerParams(vmem_limit_bytes=24 << 20),
        name="finish",
    )(own, plus, two, minus)


def shift(a, axis, by):
    n = lax.axis_size(axis)
    return lax.ppermute(a, axis, [(i, (i + by) % n) for i in range(n)])


def per_device(tokens, out_grad, expert_ids, combine_weights, w_gate, w_up, w_down):
    ids = expert_ids.T
    weights = combine_weights.T
    half = EXPERTS // 2
    place = lax.axis_index("tensor").astype(jnp.int32)[None]
    own = dispatch(place, ids, tokens, out_grad)
    own = lax.all_to_all(own, "expert", split_axis=0, concat_axis=0)

    width = own.shape[2] - PART
    blocks = {0: own}
    owns = {4: shift(own[:, :, width:], "dp", 4)}
    quarters = {}

    def spread(*dists):
        mine = jnp.concatenate([owns[d][:, :, -PART:] for d in dists], axis=0)
        others = [shift(mine, "tensor", by) for by in (1, -1, 2)]
        shaped = [a.reshape(len(dists), EXPERTS, CAP, PART) for a in others]
        quarters.update({d: (i, shaped) for i, d in enumerate(dists)})
        return others

    def hop(dist, beside):
        ahead, behind, *_ = lax.optimization_barrier((blocks[dist - 1], blocks[1 - dist], *beside))
        owns[dist] = blocks[dist] = shift(ahead, "dp", -1)
        owns[-dist] = blocks[-dist] = shift(behind, "dp", 1)

    owns[0] = own
    hop(1, [])
    hop(2, [owns[4]])
    hop(3, spread(0, 4))
    beside = spread(1, -1, 2, -2)
    low, high, *_ = lax.optimization_barrier(
        (blocks[-3][:AHEAD, :, :width], blocks[3][AHEAD:, :, :width], *beside)
    )
    split = [shift(low, "dp", 1), shift(high, "dp", -1)]
    spread(3, -3)

    grads = {}
    for dists in ((0, 1, -1, 2, -2), (3, -3, 4)):
        arrays = [blocks[d] for d in dists if d != 4] + (split if 4 in dists else [])
        found = forward(
            place,
            arrays,
            [owns[d] for d in dists],
            [quarters[d] for d in dists],
            [a for _, a in grads.values()][:1],
            w_gate,
            w_up,
            w_down,
        )
        grads.update(zip(dists, found))

    got = {0: (), half: ()}
    final = {0: {}, half: {}}
    for step in range(4):
        for first in (0, half):
            long = 1 if first == 0 else -1
            dists = [long * (4 - step)] + ([-long * (3 - step)] if step < 3 else [])
            small = [grads[4 if d == -4 else d] for d in dists]
            received = got[first][: len(dists)]
            outs = backward(first, small, received, w_gate, w_up)
            sent = [shift(o, "dp", 1 if d > 0 else -1) for o, d in zip(outs, dists)]
            got[first] = sent
            final[first].update({i: a for i, a in enumerate(sent)})
    low = [final[0][0], final[0][1]]
    high = [final[half][0], final[half][1]]
    rows = last(own_product(grads[0][0], w_gate, w_up), grads[0][1], low, high)
    rows = lax.all_to_all(rows, "expert", split_axis=0, concat_axis=0)
    part = combine(ids, weights, rows)
    x_grad, router = finish(
        part, shift(part, "tensor", 1), shift(part, "tensor", 2), shift(part, "tensor", -1)
    )
    return x_grad, router.T


def solution(mesh):
    placed = (
        P("dp", "expert"),
        P("dp", "expert"),
        P("dp", None),
        P("dp", None),
        P("expert", None, ("dp", "tensor")),
        P("expert", None, ("dp", "tensor")),
        P("expert", ("dp", "tensor"), None),
    )
    return jax.shard_map(
        per_device,
        mesh=mesh,
        in_specs=placed,
        out_specs=(P("dp", "expert"), P("dp", None)),
        check_vma=False,
    )
```

profile of v0, /device:TPU:1, one launch (start us, length us, event | category | flops | bytes accessed | tf_op | source)
XLA Modules:
  0.0 203.8 jit_solution(12942967216748528062)
XLA Ops:
  3.8 19.5 %all_to_all.10.refs_0_.refs_5_.refs_10_ = bf16[8,48,1152]{2,1,0:T(8,128)(2,1)S(1)} all-to-all(bf16[8,48,1152]{2,1,0:T(8,128)(2,1)S(1)} %dispatch.1), channel_id=1, replica_groups=mesh['dp'=8,'expert'=8,'tensor'=4] {'expert'}, dimensions={0} | all-to-all | bytes 1769472 | tf_op jit(solution)/shard_map/all_to_all | solution.py:384
  23.3 5.6 %collective-permute-start = (bf16[8,48,1152]{2,1,0:T(8,128)(2,1)S(1)}, bf16[8,48,1152]{2,1,0:T(8,128)(2,1)S(1)}, u32[]{:S(2)}, u32[]{:S(2)}) collective-permute-start(bf16[8,48,1152]{2,1,0:T(8,128)(2,1)S(1)} %all_to_all.10.refs_0_.refs_5_.refs_10_), channel_id=1, source_target_pairs={{0,224},{32,0},{64,32},{96,64},{128,96},{160,128},{192,160},{224,1... | collective-permute-start | bytes 2654216 | tf_op jit(solution)/shard_map/ppermute | solution.py:375
  28.9 2.9 %collective-permute-start.2 = (bf16[8,48,128]{2,1,0:T(8,128)(2,1)S(1)}, bf16[8,48,128]{2,1,0:T(8,128)(2,1)S(1)}, u32[]{:S(2)}, u32[]{:S(2)}) collective-permute-start(bf16[8,48,128]{2,1,0:T(8,128)(2,1)S(1)} %slice.37), channel_id=1, source_target_pairs={{0,128},{32,160},{64,192},{96,224},{128,0},{160,32},{192,64},{224,... | collective-permute-start | bytes 294920 | tf_op jit(solution)/shard_map/ppermute | solution.py:375
  31.8 22.4 %collective-permute-done.2.refs_10_ = bf16[8,48,128]{2,1,0:T(8,128)(2,1)S(1)} collective-permute-done((bf16[8,48,128]{2,1,0:T(8,128)(2,1)S(1)}, bf16[8,48,128]{2,1,0:T(8,128)(2,1)S(1)}, u32[]{:S(2)}, u32[]{:S(2)}) %collective-permute-start.2) | collective-permute-done | bytes 98336 | tf_op jit(solution)/shard_map/ppermute | solution.py:375
  55.7 2.8 %collective-permute-start.7 = (bf16[16,48,128]{2,1,0:T(8,128)(2,1)S(1)}, bf16[16,48,128]{2,1,0:T(8,128)(2,1)S(1)}, u32[]{:S(2)}, u32[]{:S(2)}) collective-permute-start(bf16[16,48,128]{2,1,0:T(8,128)(2,1)S(1)} %pad_maximum_fusion.1), channel_id=1, source_target_pairs={{0,2},{1,3},{2,0},{3,1},{4,6},{5,7},{6,4},{7,5},{8,10},{9,11},{10,... | collective-permute-start | bytes 589832 | tf_op jit(solution)/shard_map/ppermute | solution.py:375
  61.8 3.3 %collective-permute-done.6 = bf16[16,48,128]{2,1,0:T(8,128)(2,1)S(1)} collective-permute-done((bf16[16,48,128]{2,1,0:T(8,128)(2,1)S(1)}, bf16[16,48,128]{2,1,0:T(8,128)(2,1)S(1)}, u32[]{:S(2)}, u32[]{:S(2)}) %collective-permute-start.6) | collective-permute-done | bytes 196640 | tf_op jit(solution)/shard_map/ppermute | solution.py:375
  65.1 2.7 %collective-permute-done.5 = bf16[16,48,128]{2,1,0:T(8,128)(2,1)S(1)} collective-permute-done((bf16[16,48,128]{2,1,0:T(8,128)(2,1)S(1)}, bf16[16,48,128]{2,1,0:T(8,128)(2,1)S(1)}, u32[]{:S(2)}, u32[]{:S(2)}) %collective-permute-start.5) | collective-permute-done | bytes 196640 | tf_op jit(solution)/shard_map/ppermute | solution.py:375
  67.8 5.3 %collective-permute-done.3.refs_3_.refs_8_.refs_13_ = bf16[8,48,1152]{2,1,0:T(8,128)(2,1)S(1)} collective-permute-done((bf16[8,48,1152]{2,1,0:T(8,128)(2,1)S(1)}, bf16[8,48,1152]{2,1,0:T(8,128)(2,1)S(1)}, u32[]{:S(2)}, u32[]{:S(2)}) %collective-permute-start.3) | collective-permute-done | bytes 884768 | tf_op jit(solution)/shard_map/ppermute | solution.py:375
  76.7 2.8 %collective-permute-start.10 = (bf16[32,48,128]{2,1,0:T(8,128)(2,1)S(1)}, bf16[32,48,128]{2,1,0:T(8,128)(2,1)S(1)}, u32[]{:S(2)}, u32[]{:S(2)}) collective-permute-start(bf16[32,48,128]{2,1,0:T(8,128)(2,1)S(1)} %pad_maximum_fusion), channel_id=1, source_target_pairs={{0,2},{1,3},{2,0},{3,1},{4,6},{5,7},{6,4},{7,5},{8,10},{9,11},{10,... | collective-permute-start | bytes 1179656 | tf_op jit(solution)/shard_map/ppermute | solution.py:375
  81.0 12.3 %collective-permute-done.11.refs_0_.refs_4_.refs_8_ = bf16[8,48,1152]{2,1,0:T(8,128)(2,1)S(1)} collective-permute-done((bf16[8,48,1152]{2,1,0:T(8,128)(2,1)S(1)}, bf16[8,48,1152]{2,1,0:T(8,128)(2,1)S(1)}, u32[]{:S(2)}, u32[]{:S(2)}) %collective-permute-start.11) | collective-permute-done | bytes 884768 | tf_op jit(solution)/shard_map/ppermute | solution.py:375
  99.3 3.9 %collective-permute-start.17 = (bf16[16,48,128]{2,1,0:T(8,128)(2,1)S(1)}, bf16[16,48,128]{2,1,0:T(8,128)(2,1)S(1)}, u32[]{:S(2)}, u32[]{:S(2)}) collective-permute-start(bf16[16,48,128]{2,1,0:T(8,128)(2,1)S(1)} %pad_maximum_fusion.2), channel_id=1, source_target_pairs={{0,2},{1,3},{2,0},{3,1},{4,6},{5,7},{6,4},{7,5},{8,10},{9,11},{10,... | collective-permute-start | bytes 589832 | tf_op jit(solution)/shard_map/ppermute | solution.py:375
  106.6 5.6 %forward.2 = (bf16[48,512]{1,0:T(8,128)(2,1)S(1)}, f32[16,128]{1,0:T(8,128)S(1)}, bf16[48,512]{1,0:T(8,128)(2,1)S(1)}, f32[16,128]{1,0:T(8,128)S(1)}, bf16[48,51...) custom-call(s32[1]{0:T(128)} %bitcast.2.place_ref, ...), custom_call_target="tpu_custom_call" | custom-call | flops 2415919104 | bytes 9437184 | tf_op jit(solution)/shard_map/forward/pallas_call | solution.py:160
  112.6 4.8 %forward.3 = (bf16[48,512]{1,0:T(8,128)(2,1)S(1)}, f32[16,128]{1,0:T(8,128)S(1)}, bf16[48,512]{1,0:T(8,128)(2,1)S(1)}, f32[16,128]{1,0:T(8,128)S(1)}, bf16[48,51...) custom-call(s32[1]{0:T(128)} %bitcast.2.place_ref, bf16[8,48,1152]{2,1,0:T(8,128)(2,1)S(1)} %collective-permute-done.11.refs_0_.refs_4_.refs_8_, ...), custom_call_target="tpu_custom_call" | custom-call | flops 2415919104 | bytes 9437184 | tf_op jit(solution)/shard_map/forward/pallas_call | solution.py:160
  118.9 2.7 %collective-permute-start.19 = (bf16[208,768]{1,0:T(8,128)(2,1)S(1)}, bf16[208,768]{1,0:T(8,128)(2,1)S(1)}, u32[]{:S(2)}, u32[]{:S(2)}) collective-permute-start(bf16[208,768]{1,0:T(8,128)(2,1)S(1)} %get-tuple-element.65), channel_id=1, source_target_pairs={{0,224},{32,0},{64,32},{96,64},{128,96},{160,128},{192,160},{224,1... | collective-permute-start | bytes 958472 | tf_op jit(solution)/shard_map/ppermute | solution.py:375
  137.1 2.7 %collective-permute-done.20.refs_4_ = bf16[208,768]{1,0:T(8,128)(2,1)S(1)} collective-permute-done((bf16[208,768]{1,0:T(8,128)(2,1)S(1)}, bf16[208,768]{1,0:T(8,128)(2,1)S(1)}, u32[]{:S(2)}, u32[]{:S(2)}) %collective-permute-start.20) | collective-permute-done | bytes 319520 | tf_op jit(solution)/shard_map/ppermute | solution.py:375
  141.5 4.0 %collective-permute-done.27.refs_4_ = bf16[192,768]{1,0:T(8,128)(2,1)S(1)} collective-permute-done((bf16[192,768]{1,0:T(8,128)(2,1)S(1)}, bf16[192,768]{1,0:T(8,128)(2,1)S(1)}, u32[]{:S(2)}, u32[]{:S(2)}) %collective-permute-start.27) | collective-permute-done | bytes 294944 | tf_op jit(solution)/shard_map/ppermute | solution.py:375
  147.2 2.8 %collective-permute-start.29 = (bf16[192,768]{1,0:T(8,128)(2,1)S(1)}, bf16[192,768]{1,0:T(8,128)(2,1)S(1)}, u32[]{:S(2)}, u32[]{:S(2)}) collective-permute-start(bf16[192,768]{1,0:T(8,128)(2,1)S(1)} %get-tuple-element.74), channel_id=1, source_target_pairs={{0,224},{32,0},{64,32},{96,64},{128,96},{160,128},{192,160},{224,1... | collective-permute-start | bytes 884744 | tf_op jit(solution)/shard_map/ppermute | solution.py:375
  150.1 2.7 %collective-permute-start.24 = (bf16[208,768]{1,0:T(8,128)(2,1)S(1)}, bf16[208,768]{1,0:T(8,128)(2,1)S(1)}, u32[]{:S(2)}, u32[]{:S(2)}) collective-permute-start(bf16[208,768]{1,0:T(8,128)(2,1)S(1)} %get-tuple-element.69), channel_id=1, source_target_pairs={{0,224},{32,0},{64,32},{96,64},{128,96},{160,128},{192,160},{224,1... | collective-permute-start | bytes 958472 | tf_op jit(solution)/shard_map/ppermute | solution.py:375
  155.7 2.7 %collective-permute-start.30 = (bf16[192,768]{1,0:T(8,128)(2,1)S(1)}, bf16[192,768]{1,0:T(8,128)(2,1)S(1)}, u32[]{:S(2)}, u32[]{:S(2)}) collective-permute-start(bf16[192,768]{1,0:T(8,128)(2,1)S(1)} %backward.15), channel_id=1, source_target_pairs={{0,224},{32,0},{64,32},{96,64},{128,96},{160,128},{192,160},{224,1... | collective-permute-start | bytes 884744 | tf_op jit(solution)/shard_map/ppermute | solution.py:375
  158.4 2.8 %own_product.1.own_ref = f32[8,48,768]{2,1,0:T(8,128)S(1)} custom-call(bf16[48,512]{1,0:T(8,128)(2,1)S(1)} %get-tuple-element.44.g_ref, bf16[1,6144,256]{2,1,0:T(8,128)(2,1)S(1)} %copy-done, bf16[1,6144,256]{2,1,0:T(8,128)(2,1)S(1)} %copy-done.1), custom_call_target="tpu_custom_call" | custom-call | flops 805306368 | bytes 6291456 | tf_op jit(solution)/shard_map/own_product/pallas_call | solution.py:264
  161.2 4.1 %collective-permute-done.30.refs_2_ = bf16[192,768]{1,0:T(8,128)(2,1)S(1)} collective-permute-done((bf16[192,768]{1,0:T(8,128)(2,1)S(1)}, bf16[192,768]{1,0:T(8,128)(2,1)S(1)}, u32[]{:S(2)}, u32[]{:S(2)}) %collective-permute-start.30) | collective-permute-done | bytes 294944 | tf_op jit(solution)/shard_map/ppermute | solution.py:375
  165.6 21.2 %all_to_all.11.rows_ref = bf16[8,64,768]{2,1,0:T(8,128)(2,1)S(1)} all-to-all(bf16[8,64,768]{2,1,0:T(8,128)(2,1)S(1)} %last.1), channel_id=1, replica_groups=mesh['dp'=8,'expert'=8,'tensor'=4] {'expert'}, dimensions={0} | all-to-all | bytes 1572864 | tf_op jit(solution)/shard_map/all_to_all | solution.py:444
  191.4 2.9 %collective-permute-done.34.d_ref = bf16[144,768]{1,0:T(8,128)(2,1)S(1)} collective-permute-done((bf16[144,768]{1,0:T(8,128)(2,1)S(1)}, bf16[144,768]{1,0:T(8,128)(2,1)S(1)}, u32[]{:S(2)}, u32[]{:S(2)}) %collective-permute-start.34) | collective-permute-done | bytes 221216 | tf_op jit(solution)/shard_map/ppermute | solution.py:375
  196.8 6.3 %collective-permute-done.32.b_ref = bf16[144,768]{1,0:T(8,128)(2,1)S(1)} collective-permute-done((bf16[144,768]{1,0:T(8,128)(2,1)S(1)}, bf16[144,768]{1,0:T(8,128)(2,1)S(1)}, u32[]{:S(2)}, u32[]{:S(2)}) %collective-permute-start.32) | collective-permute-done | bytes 221216 | tf_op jit(solution)/shard_map/ppermute | solution.py:375
  (93 shorter events, 54.2 us)
Async XLA Ops:
  23.3 30.9 %collective-permute-start = (bf16[8,48,1152]{2,1,0:T(8,128)(2,1)S(1)}, bf16[8,48,1152]{2,1,0:T(8,128)(2,1)S(1)}, u32[]{:S(2)}, u32[]{:S(2)}) collective-permute-start(bf16[8,48,1152]{2,1,0:T(8,128)(2,1)S(1)} %all_to_all.10.refs_0_.refs_5_.refs_10_), channel_id=1, source_target_pairs={{0,224},{32,0},{64,32},{96,64},{128,96},{160,128},{192,160},{224,1... | collective-permute-start | bytes 2654216 | tf_op jit(solution)/shard_map/ppermute | solution.py:375
  28.9 25.3 %collective-permute-start.1 = (bf16[8,48,1152]{2,1,0:T(8,128)(2,1)S(1)}, bf16[8,48,1152]{2,1,0:T(8,128)(2,1)S(1)}, u32[]{:S(2)}, u32[]{:S(2)}) collective-permute-start(bf16[8,48,1152]{2,1,0:T(8,128)(2,1)S(1)} %all_to_all.10.refs_0_.refs_5_.refs_10_), channel_id=1, source_target_pairs={{0,32},{32,64},{64,96},{96,128},{128,160},{160,192},{192,224},{224... | collective-permute-start | bytes 2654216 | tf_op jit(solution)/shard_map/ppermute | solution.py:375
  28.9 25.3 %collective-permute-start.2 = (bf16[8,48,128]{2,1,0:T(8,128)(2,1)S(1)}, bf16[8,48,128]{2,1,0:T(8,128)(2,1)S(1)}, u32[]{:S(2)}, u32[]{:S(2)}) collective-permute-start(bf16[8,48,128]{2,1,0:T(8,128)(2,1)S(1)} %slice.37), channel_id=1, source_target_pairs={{0,128},{32,160},{64,192},{96,224},{128,0},{160,32},{192,64},{224,... | collective-permute-start | bytes 294920 | tf_op jit(solution)/shard_map/ppermute | solution.py:375
  54.2 18.8 %collective-permute-start.3 = (bf16[8,48,1152]{2,1,0:T(8,128)(2,1)S(1)}, bf16[8,48,1152]{2,1,0:T(8,128)(2,1)S(1)}, u32[]{:S(2)}, u32[]{:S(2)}) collective-permute-start(bf16[8,48,1152]{2,1,0:T(8,128)(2,1)S(1)} %collective-permute-done.refs_1_.refs_6_.refs_11_), channel_id=1, source_target_pairs={{0,224},{32,0},{64,32},{96,64},{128,96},{160,128},{192,160},{224,1... | collective-permute-start | bytes 2654216 | tf_op jit(solution)/shard_map/ppermute | solution.py:375
  54.7 20.4 %collective-permute-start.4 = (bf16[8,48,1152]{2,1,0:T(8,128)(2,1)S(1)}, bf16[8,48,1152]{2,1,0:T(8,128)(2,1)S(1)}, u32[]{:S(2)}, u32[]{:S(2)}) collective-permute-start(bf16[8,48,1152]{2,1,0:T(8,128)(2,1)S(1)} %collective-permute-done.1.refs_2_.refs_7_.refs_12_), channel_id=1, source_target_pairs={{0,32},{32,64},{64,96},{96,128},{128,160},{160,192},{192,224},{224... | collective-permute-start | bytes 2654216 | tf_op jit(solution)/shard_map/ppermute | solution.py:375
  75.0 18.2 %collective-permute-start.11 = (bf16[8,48,1152]{2,1,0:T(8,128)(2,1)S(1)}, bf16[8,48,1152]{2,1,0:T(8,128)(2,1)S(1)}, u32[]{:S(2)}, u32[]{:S(2)}) collective-permute-start(bf16[8,48,1152]{2,1,0:T(8,128)(2,1)S(1)} %collective-permute-done.3.refs_3_.refs_8_.refs_13_), channel_id=1, source_target_pairs={{0,224},{32,0},{64,32},{96,64},{128,96},{160,128},{192,160},{224,1... | collective-permute-start | bytes 2654216 | tf_op jit(solution)/shard_map/ppermute | solution.py:375
  75.3 19.4 %collective-permute-start.12 = (bf16[8,48,1152]{2,1,0:T(8,128)(2,1)S(1)}, bf16[8,48,1152]{2,1,0:T(8,128)(2,1)S(1)}, u32[]{:S(2)}, u32[]{:S(2)}) collective-permute-start(bf16[8,48,1152]{2,1,0:T(8,128)(2,1)S(1)} %collective-permute-done.4.refs_4_.refs_9_.refs_14_), channel_id=1, source_target_pairs={{0,32},{32,64},{64,96},{96,128},{128,160},{160,192},{192,224},{224... | collective-permute-start | bytes 2654216 | tf_op jit(solution)/shard_map/ppermute | solution.py:375
  76.7 18.1 %collective-permute-start.10 = (bf16[32,48,128]{2,1,0:T(8,128)(2,1)S(1)}, bf16[32,48,128]{2,1,0:T(8,128)(2,1)S(1)}, u32[]{:S(2)}, u32[]{:S(2)}) collective-permute-start(bf16[32,48,128]{2,1,0:T(8,128)(2,1)S(1)} %pad_maximum_fusion), channel_id=1, source_target_pairs={{0,2},{1,3},{2,0},{3,1},{4,6},{5,7},{6,4},{7,5},{8,10},{9,11},{10,... | collective-permute-start | bytes 1179656 | tf_op jit(solution)/shard_map/ppermute | solution.py:375
  79.5 17.1 %collective-permute-start.9 = (bf16[32,48,128]{2,1,0:T(8,128)(2,1)S(1)}, bf16[32,48,128]{2,1,0:T(8,128)(2,1)S(1)}, u32[]{:S(2)}, u32[]{:S(2)}) collective-permute-start(bf16[32,48,128]{2,1,0:T(8,128)(2,1)S(1)} %pad_maximum_fusion), channel_id=1, source_target_pairs={{0,3},{1,0},{2,1},{3,2},{4,7},{5,4},{6,5},{7,6},{8,11},{9,8},{10,9... | collective-permute-start | bytes 1179656 | tf_op jit(solution)/shard_map/ppermute | solution.py:375
  80.4 16.2 %collective-permute-start.8 = (bf16[32,48,128]{2,1,0:T(8,128)(2,1)S(1)}, bf16[32,48,128]{2,1,0:T(8,128)(2,1)S(1)}, u32[]{:S(2)}, u32[]{:S(2)}) collective-permute-start(bf16[32,48,128]{2,1,0:T(8,128)(2,1)S(1)} %pad_maximum_fusion), channel_id=1, source_target_pairs={{0,1},{1,2},{2,3},{3,0},{4,5},{5,6},{6,7},{7,4},{8,9},{9,10},{10,1... | collective-permute-start | bytes 1179656 | tf_op jit(solution)/shard_map/ppermute | solution.py:375
  96.6 16.0 %collective-permute-start.13 = (bf16[4,48,1024]{2,1,0:T(8,128)(2,1)S(1)}, bf16[4,48,1024]{2,1,0:T(8,128)(2,1)S(1)}, u32[]{:S(2)}, u32[]{:S(2)}) collective-permute-start(bf16[4,48,1024]{2,1,0:T(8,128)(2,1)S(1)} %slice.42), channel_id=1, source_target_pairs={{0,32},{32,64},{64,96},{96,128},{128,160},{160,192},{192,224},{224... | collective-permute-start | bytes 1179656 | tf_op jit(solution)/shard_map/ppermute | solution.py:375
  96.8 15.8 %collective-permute-start.14 = (bf16[4,48,1024]{2,1,0:T(8,128)(2,1)S(1)}, bf16[4,48,1024]{2,1,0:T(8,128)(2,1)S(1)}, u32[]{:S(2)}, u32[]{:S(2)}) collective-permute-start(bf16[4,48,1024]{2,1,0:T(8,128)(2,1)S(1)} %slice.43), channel_id=1, source_target_pairs={{0,224},{32,0},{64,32},{96,64},{128,96},{160,128},{192,160},{224,1... | collective-permute-start | bytes 1179656 | tf_op jit(solution)/shard_map/ppermute | solution.py:375
  99.3 12.9 %collective-permute-start.17 = (bf16[16,48,128]{2,1,0:T(8,128)(2,1)S(1)}, bf16[16,48,128]{2,1,0:T(8,128)(2,1)S(1)}, u32[]{:S(2)}, u32[]{:S(2)}) collective-permute-start(bf16[16,48,128]{2,1,0:T(8,128)(2,1)S(1)} %pad_maximum_fusion.2), channel_id=1, source_target_pairs={{0,2},{1,3},{2,0},{3,1},{4,6},{5,7},{6,4},{7,5},{8,10},{9,11},{10,... | collective-permute-start | bytes 589832 | tf_op jit(solution)/shard_map/ppermute | solution.py:375
  123.1 9.1 %collective-permute-start.25 = (bf16[192,768]{1,0:T(8,128)(2,1)S(1)}, bf16[192,768]{1,0:T(8,128)(2,1)S(1)}, u32[]{:S(2)}, u32[]{:S(2)}) collective-permute-start(bf16[192,768]{1,0:T(8,128)(2,1)S(1)} %get-tuple-element.70), channel_id=1, source_target_pairs={{0,224},{32,0},{64,32},{96,64},{128,96},{160,128},{192,160},{224,1... | collective-permute-start | bytes 884744 | tf_op jit(solution)/shard_map/ppermute | solution.py:375
  123.2 10.4 %collective-permute-start.26 = (bf16[192,768]{1,0:T(8,128)(2,1)S(1)}, bf16[192,768]{1,0:T(8,128)(2,1)S(1)}, u32[]{:S(2)}, u32[]{:S(2)}) collective-permute-start(bf16[192,768]{1,0:T(8,128)(2,1)S(1)} %get-tuple-element.71), channel_id=1, source_target_pairs={{0,32},{32,64},{64,96},{96,128},{128,160},{160,192},{192,224},{224... | collective-permute-start | bytes 884744 | tf_op jit(solution)/shard_map/ppermute | solution.py:375
  128.3 11.5 %collective-permute-start.20 = (bf16[208,768]{1,0:T(8,128)(2,1)S(1)}, bf16[208,768]{1,0:T(8,128)(2,1)S(1)}, u32[]{:S(2)}, u32[]{:S(2)}) collective-permute-start(bf16[208,768]{1,0:T(8,128)(2,1)S(1)} %get-tuple-element.66), channel_id=1, source_target_pairs={{0,32},{32,64},{64,96},{96,128},{128,160},{160,192},{192,224},{224... | collective-permute-start | bytes 958472 | tf_op jit(solution)/shard_map/ppermute | solution.py:375
  128.4 11.4 %collective-permute-start.21 = (bf16[208,768]{1,0:T(8,128)(2,1)S(1)}, bf16[208,768]{1,0:T(8,128)(2,1)S(1)}, u32[]{:S(2)}, u32[]{:S(2)}) collective-permute-start(bf16[208,768]{1,0:T(8,128)(2,1)S(1)} %get-tuple-element.67), channel_id=1, source_target_pairs={{0,224},{32,0},{64,32},{96,64},{128,96},{160,128},{192,160},{224,1... | collective-permute-start | bytes 958472 | tf_op jit(solution)/shard_map/ppermute | solution.py:375
  135.1 10.3 %collective-permute-start.27 = (bf16[192,768]{1,0:T(8,128)(2,1)S(1)}, bf16[192,768]{1,0:T(8,128)(2,1)S(1)}, u32[]{:S(2)}, u32[]{:S(2)}) collective-permute-start(bf16[192,768]{1,0:T(8,128)(2,1)S(1)} %get-tuple-element.72), channel_id=1, source_target_pairs={{0,224},{32,0},{64,32},{96,64},{128,96},{160,128},{192,160},{224,1... | collective-permute-start | bytes 884744 | tf_op jit(solution)/shard_map/ppermute | solution.py:375
  141.4 11.4 %collective-permute-start.22 = (bf16[208,768]{1,0:T(8,128)(2,1)S(1)}, bf16[208,768]{1,0:T(8,128)(2,1)S(1)}, u32[]{:S(2)}, u32[]{:S(2)}) collective-permute-start(bf16[208,768]{1,0:T(8,128)(2,1)S(1)} %get-tuple-element.68), channel_id=1, source_target_pairs={{0,32},{32,64},{64,96},{96,128},{128,160},{160,192},{192,224},{224... | collective-permute-start | bytes 958472 | tf_op jit(solution)/shard_map/ppermute | solution.py:375
  150.1 11.1 %collective-permute-start.31 = (bf16[192,768]{1,0:T(8,128)(2,1)S(1)}, bf16[192,768]{1,0:T(8,128)(2,1)S(1)}, u32[]{:S(2)}, u32[]{:S(2)}) collective-permute-start(bf16[192,768]{1,0:T(8,128)(2,1)S(1)} %get-tuple-element.75), channel_id=1, source_target_pairs={{0,32},{32,64},{64,96},{96,128},{128,160},{160,192},{192,224},{224... | collective-permute-start | bytes 884744 | tf_op jit(solution)/shard_map/ppermute | solution.py:375
  150.1 11.1 %collective-permute-start.24 = (bf16[208,768]{1,0:T(8,128)(2,1)S(1)}, bf16[208,768]{1,0:T(8,128)(2,1)S(1)}, u32[]{:S(2)}, u32[]{:S(2)}) collective-permute-start(bf16[208,768]{1,0:T(8,128)(2,1)S(1)} %get-tuple-element.69), channel_id=1, source_target_pairs={{0,224},{32,0},{64,32},{96,64},{128,96},{160,128},{192,160},{224,1... | collective-permute-start | bytes 958472 | tf_op jit(solution)/shard_map/ppermute | solution.py:375
  154.2 11.3 %collective-permute-start.23 = (bf16[208,768]{1,0:T(8,128)(2,1)S(1)}, bf16[208,768]{1,0:T(8,128)(2,1)S(1)}, u32[]{:S(2)}, u32[]{:S(2)}) collective-permute-start(bf16[208,768]{1,0:T(8,128)(2,1)S(1)} %backward.11), channel_id=1, source_target_pairs={{0,32},{32,64},{64,96},{96,128},{128,160},{160,192},{192,224},{224... | collective-permute-start | bytes 958472 | tf_op jit(solution)/shard_map/ppermute | solution.py:375
  155.7 9.6 %collective-permute-start.30 = (bf16[192,768]{1,0:T(8,128)(2,1)S(1)}, bf16[192,768]{1,0:T(8,128)(2,1)S(1)}, u32[]{:S(2)}, u32[]{:S(2)}) collective-permute-start(bf16[192,768]{1,0:T(8,128)(2,1)S(1)} %backward.15), channel_id=1, source_target_pairs={{0,224},{32,0},{64,32},{96,64},{128,96},{160,128},{192,160},{224,1... | collective-permute-start | bytes 884744 | tf_op jit(solution)/shard_map/ppermute | solution.py:375
  191.4 11.6 %collective-permute-start.32 = (bf16[144,768]{1,0:T(8,128)(2,1)S(1)}, bf16[144,768]{1,0:T(8,128)(2,1)S(1)}, u32[]{:S(2)}, u32[]{:S(2)}) collective-permute-start(bf16[144,768]{1,0:T(8,128)(2,1)S(1)} %combine.1.a_ref), channel_id=1, source_target_pairs={{0,1},{1,2},{2,3},{3,0},{4,5},{5,6},{6,7},{7,4},{8,9},{9,10},{10,1... | collective-permute-start | bytes 663560 | tf_op jit(solution)/shard_map/ppermute | solution.py:375
  (20 other events, 347.1 us)
where the time goes:
time: 204 us
  waiting for transfers between devices  80.8 us (40%)
  starting transfers between devices  49.4 us (24%)
  blocking collectives  40.7 us (20%)
  Pallas kernels  27.3 us (13%)
  local copies, waits for them, and re-layouts  4.64 us (2%)
    ppermute x35, waiting for transfers between devices, shift(): return lax.ppermute(a, axis, [(i, (i + by) % n) for i in range(n)])  80.8 us
    ppermute x35, starting transfers between devices, shift(): return lax.ppermute(a, axis, [(i, (i + by) % n) for i in range(n)])  49.4 us
    all_to_all x1, blocking collectives, per_device(): rows = lax.all_to_all(rows, 'expert', split_axis=0, concat_axis=0)  21.2 us
    all_to_all x1, blocking collectives, per_device(): own = lax.all_to_all(own, 'expert', split_axis=0, concat_axis=0)  19.5 us
    pallas_call x8, Pallas kernels, backward(): pl.pallas_call(functools.partial(backward_kernel, ways, bool(received), f...  11.9 us
    pallas_call x2, Pallas kernels, forward(): pl.pallas_call(functools.partial(forward_kernel, count, split, len(after)...  10.4 us
    unnamed x18, local copies, waits for them, and re-layouts  4.44 us
  transfers between devices with their start and end apart: 35, of which 21 were waited for; matrix products, arithmetic and copies ran while one was open for 0% of the time, Pallas kernels for 9%

commit v1 on v0

--- a/solution.py
+++ b/solution.py
@@ -279,13 +279,19 @@
     low, high, out_ref = refs[0:2], refs[2:4], refs[4]
     half = EXPERTS // 2
     total = s_ref[0:1, :] + (unpack_slots(low[0][0:16, 0:128]) + unpack_slots(low[1][0:16, 0:128]))
-    tail = pack_slots(total, out_ref.shape[2])
+    width = own_ref.shape[2]
+    row = lax.broadcasted_iota(jnp.int32, (CAP, 128), 0)
+    column = lax.broadcasted_iota(jnp.int32, (CAP, 128), 1)
+    total = jnp.sum(jnp.where(row == column, total, 0.0), axis=1, keepdims=True)
+    high_part = total.astype(BF).astype(F32)
+    tail = jnp.where(column == 0, high_part, jnp.where(column == 1, total - high_part, 0.0))
+    tail = tail.astype(BF)
     for e in range(EXPERTS):
         parts, start = (low, 16 + e * CAP) if e < half else (high, (e - half) * CAP)
         rows = slice(start, start + CAP)
         sums = parts[0][rows, :].astype(F32) + parts[1][rows, :].astype(F32)
-        out_ref[e, 0:CAP, :] = (own_ref[e] + sums).astype(BF)
-        out_ref[e, CAP : CAP + 16, :] = tail
+        out_ref[e, :, 0:width] = (own_ref[e] + sums).astype(BF)
+        out_ref[e, :, width:] = tail
 
 
 def last(own, slots, low, high):
@@ -293,7 +299,7 @@
     return pl.pallas_call(
         last_kernel,
         in_specs=[pl.BlockSpec(memory_space=pltpu.VMEM)] * len(operands),
-        out_shape=jax.ShapeDtypeStruct((EXPERTS, CAP + 16, own.shape[2]), BF),
+        out_shape=jax.ShapeDtypeStruct((EXPERTS, CAP, own.shape[2] + 128), BF),
         compiler_params=pltpu.CompilerParams(vmem_limit_bytes=24 << 20),
         name="last",
     )(*operands)
@@ -302,23 +308,22 @@
 def combine_kernel(ids_ref, weight_ref, rows_ref, out_ref):
     ind0, ind1, count = slot_masks(ids_ref[...])
     tokens = ind0.shape[1]
-    width = rows_ref.shape[2]
+    width = rows_ref.shape[2] - 128
     weights = weight_ref[...]
     scale = ind0 * weights[0:1, :] + ind1 * weights[1:2, :]
     slots = lax.broadcasted_iota(jnp.int32, (CAP, tokens), 0)
     picks = []
-    router0 = jnp.zeros((16, tokens), F32)
-    router1 = jnp.zeros((16, tokens), F32)
+    ones0, ones1 = [], []
     for e in range(EXPERTS):
         here = count[e : e + 1, :] == slots
         picks.append(jnp.where(here, scale[e : e + 1, :], 0.0))
-        slot_rows = rows_ref[e, CAP : CAP + 16, 0:128][:, :CAP]
-        one0 = jnp.where(here, ind0[e : e + 1, :], 0.0).astype(BF)
-        one1 = jnp.where(here, ind1[e : e + 1, :], 0.0).astype(BF)
-        router0 += jnp.dot(slot_rows, one0, preferred_element_type=F32)
-        router1 += jnp.dot(slot_rows, one1, preferred_element_type=F32)
+        ones0.append(jnp.where(here, ind0[e : e + 1, :], 0.0).astype(BF))
+        ones1.append(jnp.where(here, ind1[e : e + 1, :], 0.0).astype(BF))
+    sums = jnp.concatenate([rows_ref[e, :, width:] for e in range(EXPERTS)], axis=0)
+    router0 = tn(sums, jnp.concatenate(ones0, axis=0))
+    router1 = tn(sums, jnp.concatenate(ones1, axis=0))
     rest = jnp.concatenate(picks, axis=0)
-    rows = jnp.concatenate([rows_ref[e, 0:CAP, :] for e in range(EXPERTS)], axis=0)
+    rows = jnp.concatenate([rows_ref[e, :, 0:width] for e in range(EXPERTS)], axis=0)
     total = jnp.zeros((tokens, width), F32)
     for _ in range(3):
         part = rest.astype(BF)
@@ -340,7 +345,7 @@
     tokens = ids.shape[1]
     return pl.pallas_call(
         combine_kernel,
-        out_shape=jax.ShapeDtypeStruct((tokens + 16, rows.shape[2]), BF),
+        out_shape=jax.ShapeDtypeStruct((tokens + 16, rows.shape[2] - 128), BF),
         compiler_params=pltpu.CompilerParams(vmem_limit_bytes=24 << 20),
         name="combine",
     )(ids, weights, rows)
@@ -429,7 +434,7 @@
     got = {0: (), half: ()}
     final = {0: {}, half: {}}
     for step in range(4):
-        for first in (0, half):
+        for first in ((0, half) if step % 2 == 0 else (half, 0)):
             long = 1 if first == 0 else -1
             dists = [long * (4 - step)] + ([-long * (3 - step)] if step < 3 else [])
             small = [grads[4 if d == -4 else d] for d in dists]

time: 204 us -> 203 us (level)
  no operation moved by 1% of the time
where the time goes in v1:
time: 203 us
  waiting for transfers between devices  80.9 us (40%)
  starting transfers between devices  49.4 us (24%)
  blocking collectives  39.7 us (20%)
  Pallas kernels  27.3 us (13%)
  local copies, waits for them, and re-layouts  4.64 us (2%)
    ppermute x35, waiting for transfers between devices, shift(): return lax.ppermute(a, axis, [(i, (i + by) % n) for i in range(n)])  80.9 us
    ppermute x35, starting transfers between devices, shift(): return lax.ppermute(a, axis, [(i, (i + by) % n) for i in range(n)])  49.4 us
    all_to_all x1, blocking collectives, per_device(): rows = lax.all_to_all(rows, 'expert', split_axis=0, concat_axis=0)  20.2 us
    all_to_all x1, blocking collectives, per_device(): own = lax.all_to_all(own, 'expert', split_axis=0, concat_axis=0)  19.5 us
    pallas_call x8, Pallas kernels, backward(): pl.pallas_call(functools.partial(backward_kernel, ways, bool(received), f...  11.9 us
    pallas_call x2, Pallas kernels, forward(): pl.pallas_call(functools.partial(forward_kernel, count, split, len(after)...  10.4 us
    unnamed x18, local copies, waits for them, and re-layouts  4.44 us
  transfers between devices with their start and end apart: 35, of which 21 were waited for; matrix products, arithmetic and copies ran while one was open for 0% of the time, Pallas kernels for 9%

profile of v1, /device:TPU:1, one launch (start us, length us, event | category | flops | bytes accessed | tf_op | source)
XLA Modules:
  0.0 203.0 jit_solution(8188276899356974632)
XLA Ops:
  3.8 19.5 %all_to_all.10.refs_0_.refs_5_.refs_10_ = bf16[8,48,1152]{2,1,0:T(8,128)(2,1)S(1)} all-to-all(bf16[8,48,1152]{2,1,0:T(8,128)(2,1)S(1)} %dispatch.1), channel_id=1, replica_groups=mesh['dp'=8,'expert'=8,'tensor'=4] {'expert'}, dimensions={0} | all-to-all | bytes 1769472 | tf_op jit(solution)/shard_map/all_to_all | solution.py:389
  23.3 5.6 %collective-permute-start = (bf16[8,48,1152]{2,1,0:T(8,128)(2,1)S(1)}, bf16[8,48,1152]{2,1,0:T(8,128)(2,1)S(1)}, u32[]{:S(2)}, u32[]{:S(2)}) collective-permute-start(bf16[8,48,1152]{2,1,0:T(8,128)(2,1)S(1)} %all_to_all.10.refs_0_.refs_5_.refs_10_), channel_id=1, source_target_pairs={{0,224},{32,0},{64,32},{96,64},{128,96},{160,128},{192,160},{224,1... | collective-permute-start | bytes 2654216 | tf_op jit(solution)/shard_map/ppermute | solution.py:380
  28.9 2.9 %collective-permute-start.2 = (bf16[8,48,128]{2,1,0:T(8,128)(2,1)S(1)}, bf16[8,48,128]{2,1,0:T(8,128)(2,1)S(1)}, u32[]{:S(2)}, u32[]{:S(2)}) collective-permute-start(bf16[8,48,128]{2,1,0:T(8,128)(2,1)S(1)} %slice.37), channel_id=1, source_target_pairs={{0,128},{32,160},{64,192},{96,224},{128,0},{160,32},{192,64},{224,... | collective-permute-start | bytes 294920 | tf_op jit(solution)/shard_map/ppermute | solution.py:380
  31.8 22.4 %collective-permute-done.2.refs_10_ = bf16[8,48,128]{2,1,0:T(8,128)(2,1)S(1)} collective-permute-done((bf16[8,48,128]{2,1,0:T(8,128)(2,1)S(1)}, bf16[8,48,128]{2,1,0:T(8,128)(2,1)S(1)}, u32[]{:S(2)}, u32[]{:S(2)}) %collective-permute-start.2) | collective-permute-done | bytes 98336 | tf_op jit(solution)/shard_map/ppermute | solution.py:380
  55.7 2.8 %collective-permute-start.7 = (bf16[16,48,128]{2,1,0:T(8,128)(2,1)S(1)}, bf16[16,48,128]{2,1,0:T(8,128)(2,1)S(1)}, u32[]{:S(2)}, u32[]{:S(2)}) collective-permute-start(bf16[16,48,128]{2,1,0:T(8,128)(2,1)S(1)} %pad_maximum_fusion.1), channel_id=1, source_target_pairs={{0,2},{1,3},{2,0},{3,1},{4,6},{5,7},{6,4},{7,5},{8,10},{9,11},{10,... | collective-permute-start | bytes 589832 | tf_op jit(solution)/shard_map/ppermute | solution.py:380
  61.8 3.3 %collective-permute-done.6 = bf16[16,48,128]{2,1,0:T(8,128)(2,1)S(1)} collective-permute-done((bf16[16,48,128]{2,1,0:T(8,128)(2,1)S(1)}, bf16[16,48,128]{2,1,0:T(8,128)(2,1)S(1)}, u32[]{:S(2)}, u32[]{:S(2)}) %collective-permute-start.6) | collective-permute-done | bytes 196640 | tf_op jit(solution)/shard_map/ppermute | solution.py:380
  65.1 2.7 %collective-permute-done.5 = bf16[16,48,128]{2,1,0:T(8,128)(2,1)S(1)} collective-permute-done((bf16[16,48,128]{2,1,0:T(8,128)(2,1)S(1)}, bf16[16,48,128]{2,1,0:T(8,128)(2,1)S(1)}, u32[]{:S(2)}, u32[]{:S(2)}) %collective-permute-start.5) | collective-permute-done | bytes 196640 | tf_op jit(solution)/shard_map/ppermute | solution.py:380
  67.8 5.3 %collective-permute-done.3.refs_3_.refs_8_.refs_13_ = bf16[8,48,1152]{2,1,0:T(8,128)(2,1)S(1)} collective-permute-done((bf16[8,48,1152]{2,1,0:T(8,128)(2,1)S(1)}, bf16[8,48,1152]{2,1,0:T(8,128)(2,1)S(1)}, u32[]{:S(2)}, u32[]{:S(2)}) %collective-permute-start.3) | collective-permute-done | bytes 884768 | tf_op jit(solution)/shard_map/ppermute | solution.py:380
  76.7 2.8 %collective-permute-start.10 = (bf16[32,48,128]{2,1,0:T(8,128)(2,1)S(1)}, bf16[32,48,128]{2,1,0:T(8,128)(2,1)S(1)}, u32[]{:S(2)}, u32[]{:S(2)}) collective-permute-start(bf16[32,48,128]{2,1,0:T(8,128)(2,1)S(1)} %pad_maximum_fusion), channel_id=1, source_target_pairs={{0,2},{1,3},{2,0},{3,1},{4,6},{5,7},{6,4},{7,5},{8,10},{9,11},{10,... | collective-permute-start | bytes 1179656 | tf_op jit(solution)/shard_map/ppermute | solution.py:380
  81.0 12.3 %collective-permute-done.11.refs_0_.refs_4_.refs_8_ = bf16[8,48,1152]{2,1,0:T(8,128)(2,1)S(1)} collective-permute-done((bf16[8,48,1152]{2,1,0:T(8,128)(2,1)S(1)}, bf16[8,48,1152]{2,1,0:T(8,128)(2,1)S(1)}, u32[]{:S(2)}, u32[]{:S(2)}) %collective-permute-start.11) | collective-permute-done | bytes 884768 | tf_op jit(solution)/shard_map/ppermute | solution.py:380
  99.3 3.9 %collective-permute-start.17 = (bf16[16,48,128]{2,1,0:T(8,128)(2,1)S(1)}, bf16[16,48,128]{2,1,0:T(8,128)(2,1)S(1)}, u32[]{:S(2)}, u32[]{:S(2)}) collective-permute-start(bf16[16,48,128]{2,1,0:T(8,128)(2,1)S(1)} %pad_maximum_fusion.2), channel_id=1, source_target_pairs={{0,2},{1,3},{2,0},{3,1},{4,6},{5,7},{6,4},{7,5},{8,10},{9,11},{10,... | collective-permute-start | bytes 589832 | tf_op jit(solution)/shard_map/ppermute | solution.py:380
  106.6 5.6 %forward.2 = (bf16[48,512]{1,0:T(8,128)(2,1)S(1)}, f32[16,128]{1,0:T(8,128)S(1)}, bf16[48,512]{1,0:T(8,128)(2,1)S(1)}, f32[16,128]{1,0:T(8,128)S(1)}, bf16[48,51...) custom-call(s32[1]{0:T(128)} %bitcast.2.place_ref, ...), custom_call_target="tpu_custom_call" | custom-call | flops 2415919104 | bytes 9437184 | tf_op jit(solution)/shard_map/forward/pallas_call | solution.py:160
  112.6 4.8 %forward.3 = (bf16[48,512]{1,0:T(8,128)(2,1)S(1)}, f32[16,128]{1,0:T(8,128)S(1)}, bf16[48,512]{1,0:T(8,128)(2,1)S(1)}, f32[16,128]{1,0:T(8,128)S(1)}, bf16[48,51...) custom-call(s32[1]{0:T(128)} %bitcast.2.place_ref, bf16[8,48,1152]{2,1,0:T(8,128)(2,1)S(1)} %collective-permute-done.11.refs_0_.refs_4_.refs_8_, ...), custom_call_target="tpu_custom_call" | custom-call | flops 2415919104 | bytes 9437184 | tf_op jit(solution)/shard_map/forward/pallas_call | solution.py:160
  128.4 2.7 %collective-permute-start.21 = (bf16[208,768]{1,0:T(8,128)(2,1)S(1)}, bf16[208,768]{1,0:T(8,128)(2,1)S(1)}, u32[]{:S(2)}, u32[]{:S(2)}) collective-permute-start(bf16[208,768]{1,0:T(8,128)(2,1)S(1)} %get-tuple-element.67), channel_id=1, source_target_pairs={{0,224},{32,0},{64,32},{96,64},{128,96},{160,128},{192,160},{224,1... | collective-permute-start | bytes 958472 | tf_op jit(solution)/shard_map/ppermute | solution.py:380
  137.1 2.7 %collective-permute-done.20.refs_4_ = bf16[208,768]{1,0:T(8,128)(2,1)S(1)} collective-permute-done((bf16[208,768]{1,0:T(8,128)(2,1)S(1)}, bf16[208,768]{1,0:T(8,128)(2,1)S(1)}, u32[]{:S(2)}, u32[]{:S(2)}) %collective-permute-start.20) | collective-permute-done | bytes 319520 | tf_op jit(solution)/shard_map/ppermute | solution.py:380
  141.5 4.0 %collective-permute-done.27.refs_4_ = bf16[192,768]{1,0:T(8,128)(2,1)S(1)} collective-permute-done((bf16[192,768]{1,0:T(8,128)(2,1)S(1)}, bf16[192,768]{1,0:T(8,128)(2,1)S(1)}, u32[]{:S(2)}, u32[]{:S(2)}) %collective-permute-start.27) | collective-permute-done | bytes 294944 | tf_op jit(solution)/shard_map/ppermute | solution.py:380
  147.2 2.8 %collective-permute-start.29 = (bf16[192,768]{1,0:T(8,128)(2,1)S(1)}, bf16[192,768]{1,0:T(8,128)(2,1)S(1)}, u32[]{:S(2)}, u32[]{:S(2)}) collective-permute-start(bf16[192,768]{1,0:T(8,128)(2,1)S(1)} %get-tuple-element.74), channel_id=1, source_target_pairs={{0,224},{32,0},{64,32},{96,64},{128,96},{160,128},{192,160},{224,1... | collective-permute-start | bytes 884744 | tf_op jit(solution)/shard_map/ppermute | solution.py:380
  150.1 2.7 %collective-permute-start.24 = (bf16[208,768]{1,0:T(8,128)(2,1)S(1)}, bf16[208,768]{1,0:T(8,128)(2,1)S(1)}, u32[]{:S(2)}, u32[]{:S(2)}) collective-permute-start(bf16[208,768]{1,0:T(8,128)(2,1)S(1)} %get-tuple-element.69), channel_id=1, source_target_pairs={{0,224},{32,0},{64,32},{96,64},{128,96},{160,128},{192,160},{224,1... | collective-permute-start | bytes 958472 | tf_op jit(solution)/shard_map/ppermute | solution.py:380
  155.7 2.7 %collective-permute-start.30 = (bf16[192,768]{1,0:T(8,128)(2,1)S(1)}, bf16[192,768]{1,0:T(8,128)(2,1)S(1)}, u32[]{:S(2)}, u32[]{:S(2)}) collective-permute-start(bf16[192,768]{1,0:T(8,128)(2,1)S(1)} %backward.15), channel_id=1, source_target_pairs={{0,224},{32,0},{64,32},{96,64},{128,96},{160,128},{192,160},{224,1... | collective-permute-start | bytes 884744 | tf_op jit(solution)/shard_map/ppermute | solution.py:380
  158.4 2.8 %own_product.1.own_ref = f32[8,48,768]{2,1,0:T(8,128)S(1)} custom-call(bf16[48,512]{1,0:T(8,128)(2,1)S(1)} %get-tuple-element.44.g_ref, bf16[1,6144,256]{2,1,0:T(8,128)(2,1)S(1)} %copy-done, bf16[1,6144,256]{2,1,0:T(8,128)(2,1)S(1)} %copy-done.1), custom_call_target="tpu_custom_call" | custom-call | flops 805306368 | bytes 6291456 | tf_op jit(solution)/shard_map/own_product/pallas_call | solution.py:264
  161.2 4.1 %collective-permute-done.30.refs_2_ = bf16[192,768]{1,0:T(8,128)(2,1)S(1)} collective-permute-done((bf16[192,768]{1,0:T(8,128)(2,1)S(1)}, bf16[192,768]{1,0:T(8,128)(2,1)S(1)}, u32[]{:S(2)}, u32[]{:S(2)}) %collective-permute-start.30) | collective-permute-done | bytes 294944 | tf_op jit(solution)/shard_map/ppermute | solution.py:380
  165.7 20.2 %all_to_all.11.rows_ref = bf16[8,48,896]{2,1,0:T(8,128)(2,1)S(1)} all-to-all(bf16[8,48,896]{2,1,0:T(8,128)(2,1)S(1)} %last.1), channel_id=1, replica_groups=mesh['dp'=8,'expert'=8,'tensor'=4] {'expert'}, dimensions={0} | all-to-all | bytes 1376256 | tf_op jit(solution)/shard_map/all_to_all | solution.py:449
  190.5 3.1 %collective-permute-done.34.d_ref = bf16[144,768]{1,0:T(8,128)(2,1)S(1)} collective-permute-done((bf16[144,768]{1,0:T(8,128)(2,1)S(1)}, bf16[144,768]{1,0:T(8,128)(2,1)S(1)}, u32[]{:S(2)}, u32[]{:S(2)}) %collective-permute-start.34) | collective-permute-done | bytes 221216 | tf_op jit(solution)/shard_map/ppermute | solution.py:380
  195.9 6.3 %collective-permute-done.32.b_ref = bf16[144,768]{1,0:T(8,128)(2,1)S(1)} collective-permute-done((bf16[144,768]{1,0:T(8,128)(2,1)S(1)}, bf16[144,768]{1,0:T(8,128)(2,1)S(1)}, u32[]{:S(2)}, u32[]{:S(2)}) %collective-permute-start.32) | collective-permute-done | bytes 221216 | tf_op jit(solution)/shard_map/ppermute | solution.py:380
  (93 shorter events, 54.2 us)
Async XLA Ops:
  23.3 30.9 %collective-permute-start = (bf16[8,48,1152]{2,1,0:T(8,128)(2,1)S(1)}, bf16[8,48,1152]{2,1,0:T(8,128)(2,1)S(1)}, u32[]{:S(2)}, u32[]{:S(2)}) collective-permute-start(bf16[8,48,1152]{2,1,0:T(8,128)(2,1)S(1)} %all_to_all.10.refs_0_.refs_5_.refs_10_), channel_id=1, source_target_pairs={{0,224},{32,0},{64,32},{96,64},{128,96},{160,128},{192,160},{224,1... | collective-permute-start | bytes 2654216 | tf_op jit(solution)/shard_map/ppermute | solution.py:380
  28.9 25.3 %collective-permute-start.1 = (bf16[8,48,1152]{2,1,0:T(8,128)(2,1)S(1)}, bf16[8,48,1152]{2,1,0:T(8,128)(2,1)S(1)}, u32[]{:S(2)}, u32[]{:S(2)}) collective-permute-start(bf16[8,48,1152]{2,1,0:T(8,128)(2,1)S(1)} %all_to_all.10.refs_0_.refs_5_.refs_10_), channel_id=1, source_target_pairs={{0,32},{32,64},{64,96},{96,128},{128,160},{160,192},{192,224},{224... | collective-permute-start | bytes 2654216 | tf_op jit(solution)/shard_map/ppermute | solution.py:380
  28.9 25.3 %collective-permute-start.2 = (bf16[8,48,128]{2,1,0:T(8,128)(2,1)S(1)}, bf16[8,48,128]{2,1,0:T(8,128)(2,1)S(1)}, u32[]{:S(2)}, u32[]{:S(2)}) collective-permute-start(bf16[8,48,128]{2,1,0:T(8,128)(2,1)S(1)} %slice.37), channel_id=1, source_target_pairs={{0,128},{32,160},{64,192},{96,224},{128,0},{160,32},{192,64},{224,... | collective-permute-start | bytes 294920 | tf_op jit(solution)/shard_map/ppermute | solution.py:380
  54.2 18.8 %collective-permute-start.3 = (bf16[8,48,1152]{2,1,0:T(8,128)(2,1)S(1)}, bf16[8,48,1152]{2,1,0:T(8,128)(2,1)S(1)}, u32[]{:S(2)}, u32[]{:S(2)}) collective-permute-start(bf16[8,48,1152]{2,1,0:T(8,128)(2,1)S(1)} %collective-permute-done.refs_1_.refs_6_.refs_11_), channel_id=1, source_target_pairs={{0,224},{32,0},{64,32},{96,64},{128,96},{160,128},{192,160},{224,1... | collective-permute-start | bytes 2654216 | tf_op jit(solution)/shard_map/ppermute | solution.py:380
  54.7 20.4 %collective-permute-start.4 = (bf16[8,48,1152]{2,1,0:T(8,128)(2,1)S(1)}, bf16[8,48,1152]{2,1,0:T(8,128)(2,1)S(1)}, u32[]{:S(2)}, u32[]{:S(2)}) collective-permute-start(bf16[8,48,1152]{2,1,0:T(8,128)(2,1)S(1)} %collective-permute-done.1.refs_2_.refs_7_.refs_12_), channel_id=1, source_target_pairs={{0,32},{32,64},{64,96},{96,128},{128,160},{160,192},{192,224},{224... | collective-permute-start | bytes 2654216 | tf_op jit(solution)/shard_map/ppermute | solution.py:380
  75.0 18.2 %collective-permute-start.11 = (bf16[8,48,1152]{2,1,0:T(8,128)(2,1)S(1)}, bf16[8,48,1152]{2,1,0:T(8,128)(2,1)S(1)}, u32[]{:S(2)}, u32[]{:S(2)}) collective-permute-start(bf16[8,48,1152]{2,1,0:T(8,128)(2,1)S(1)} %collective-permute-done.3.refs_3_.refs_8_.refs_13_), channel_id=1, source_target_pairs={{0,224},{32,0},{64,32},{96,64},{128,96},{160,128},{192,160},{224,1... | collective-permute-start | bytes 2654216 | tf_op jit(solution)/shard_map/ppermute | solution.py:380
  75.3 19.4 %collective-permute-start.12 = (bf16[8,48,1152]{2,1,0:T(8,128)(2,1)S(1)}, bf16[8,48,1152]{2,1,0:T(8,128)(2,1)S(1)}, u32[]{:S(2)}, u32[]{:S(2)}) collective-permute-start(bf16[8,48,1152]{2,1,0:T(8,128)(2,1)S(1)} %collective-permute-done.4.refs_4_.refs_9_.refs_14_), channel_id=1, source_target_pairs={{0,32},{32,64},{64,96},{96,128},{128,160},{160,192},{192,224},{224... | collective-permute-start | bytes 2654216 | tf_op jit(solution)/shard_map/ppermute | solution.py:380
  76.7 18.1 %collective-permute-start.10 = (bf16[32,48,128]{2,1,0:T(8,128)(2,1)S(1)}, bf16[32,48,128]{2,1,0:T(8,128)(2,1)S(1)}, u32[]{:S(2)}, u32[]{:S(2)}) collective-permute-start(bf16[32,48,128]{2,1,0:T(8,128)(2,1)S(1)} %pad_maximum_fusion), channel_id=1, source_target_pairs={{0,2},{1,3},{2,0},{3,1},{4,6},{5,7},{6,4},{7,5},{8,10},{9,11},{10,... | collective-permute-start | bytes 1179656 | tf_op jit(solution)/shard_map/ppermute | solution.py:380
  79.5 17.1 %collective-permute-start.9 = (bf16[32,48,128]{2,1,0:T(8,128)(2,1)S(1)}, bf16[32,48,128]{2,1,0:T(8,128)(2,1)S(1)}, u32[]{:S(2)}, u32[]{:S(2)}) collective-permute-start(bf16[32,48,128]{2,1,0:T(8,128)(2,1)S(1)} %pad_maximum_fusion), channel_id=1, source_target_pairs={{0,3},{1,0},{2,1},{3,2},{4,7},{5,4},{6,5},{7,6},{8,11},{9,8},{10,9... | collective-permute-start | bytes 1179656 | tf_op jit(solution)/shard_map/ppermute | solution.py:380
  80.4 16.2 %collective-permute-start.8 = (bf16[32,48,128]{2,1,0:T(8,128)(2,1)S(1)}, bf16[32,48,128]{2,1,0:T(8,128)(2,1)S(1)}, u32[]{:S(2)}, u32[]{:S(2)}) collective-permute-start(bf16[32,48,128]{2,1,0:T(8,128)(2,1)S(1)} %pad_maximum_fusion), channel_id=1, source_target_pairs={{0,1},{1,2},{2,3},{3,0},{4,5},{5,6},{6,7},{7,4},{8,9},{9,10},{10,1... | collective-permute-start | bytes 1179656 | tf_op jit(solution)/shard_map/ppermute | solution.py:380
  96.6 16.0 %collective-permute-start.13 = (bf16[4,48,1024]{2,1,0:T(8,128)(2,1)S(1)}, bf16[4,48,1024]{2,1,0:T(8,128)(2,1)S(1)}, u32[]{:S(2)}, u32[]{:S(2)}) collective-permute-start(bf16[4,48,1024]{2,1,0:T(8,128)(2,1)S(1)} %slice.42), channel_id=1, source_target_pairs={{0,32},{32,64},{64,96},{96,128},{128,160},{160,192},{192,224},{224... | collective-permute-start | bytes 1179656 | tf_op jit(solution)/shard_map/ppermute | solution.py:380
  96.8 15.8 %collective-permute-start.14 = (bf16[4,48,1024]{2,1,0:T(8,128)(2,1)S(1)}, bf16[4,48,1024]{2,1,0:T(8,128)(2,1)S(1)}, u32[]{:S(2)}, u32[]{:S(2)}) collective-permute-start(bf16[4,48,1024]{2,1,0:T(8,128)(2,1)S(1)} %slice.43), channel_id=1, source_target_pairs={{0,224},{32,0},{64,32},{96,64},{128,96},{160,128},{192,160},{224,1... | collective-permute-start | bytes 1179656 | tf_op jit(solution)/shard_map/ppermute | solution.py:380
  99.3 12.9 %collective-permute-start.17 = (bf16[16,48,128]{2,1,0:T(8,128)(2,1)S(1)}, bf16[16,48,128]{2,1,0:T(8,128)(2,1)S(1)}, u32[]{:S(2)}, u32[]{:S(2)}) collective-permute-start(bf16[16,48,128]{2,1,0:T(8,128)(2,1)S(1)} %pad_maximum_fusion.2), channel_id=1, source_target_pairs={{0,2},{1,3},{2,0},{3,1},{4,6},{5,7},{6,4},{7,5},{8,10},{9,11},{10,... | collective-permute-start | bytes 589832 | tf_op jit(solution)/shard_map/ppermute | solution.py:380
  123.1 9.1 %collective-permute-start.25 = (bf16[192,768]{1,0:T(8,128)(2,1)S(1)}, bf16[192,768]{1,0:T(8,128)(2,1)S(1)}, u32[]{:S(2)}, u32[]{:S(2)}) collective-permute-start(bf16[192,768]{1,0:T(8,128)(2,1)S(1)} %get-tuple-element.70), channel_id=1, source_target_pairs={{0,224},{32,0},{64,32},{96,64},{128,96},{160,128},{192,160},{224,1... | collective-permute-start | bytes 884744 | tf_op jit(solution)/shard_map/ppermute | solution.py:380
  123.2 10.4 %collective-permute-start.26 = (bf16[192,768]{1,0:T(8,128)(2,1)S(1)}, bf16[192,768]{1,0:T(8,128)(2,1)S(1)}, u32[]{:S(2)}, u32[]{:S(2)}) collective-permute-start(bf16[192,768]{1,0:T(8,128)(2,1)S(1)} %get-tuple-element.71), channel_id=1, source_target_pairs={{0,32},{32,64},{64,96},{96,128},{128,160},{160,192},{192,224},{224... | collective-permute-start | bytes 884744 | tf_op jit(solution)/shard_map/ppermute | solution.py:380
  128.3 11.5 %collective-permute-start.20 = (bf16[208,768]{1,0:T(8,128)(2,1)S(1)}, bf16[208,768]{1,0:T(8,128)(2,1)S(1)}, u32[]{:S(2)}, u32[]{:S(2)}) collective-permute-start(bf16[208,768]{1,0:T(8,128)(2,1)S(1)} %get-tuple-element.66), channel_id=1, source_target_pairs={{0,32},{32,64},{64,96},{96,128},{128,160},{160,192},{192,224},{224... | collective-permute-start | bytes 958472 | tf_op jit(solution)/shard_map/ppermute | solution.py:380
  128.4 11.4 %collective-permute-start.21 = (bf16[208,768]{1,0:T(8,128)(2,1)S(1)}, bf16[208,768]{1,0:T(8,128)(2,1)S(1)}, u32[]{:S(2)}, u32[]{:S(2)}) collective-permute-start(bf16[208,768]{1,0:T(8,128)(2,1)S(1)} %get-tuple-element.67), channel_id=1, source_target_pairs={{0,224},{32,0},{64,32},{96,64},{128,96},{160,128},{192,160},{224,1... | collective-permute-start | bytes 958472 | tf_op jit(solution)/shard_map/ppermute | solution.py:380
  135.1 10.3 %collective-permute-start.27 = (bf16[192,768]{1,0:T(8,128)(2,1)S(1)}, bf16[192,768]{1,0:T(8,128)(2,1)S(1)}, u32[]{:S(2)}, u32[]{:S(2)}) collective-permute-start(bf16[192,768]{1,0:T(8,128)(2,1)S(1)} %get-tuple-element.72), channel_id=1, source_target_pairs={{0,224},{32,0},{64,32},{96,64},{128,96},{160,128},{192,160},{224,1... | collective-permute-start | bytes 884744 | tf_op jit(solution)/shard_map/ppermute | solution.py:380
  141.4 11.4 %collective-permute-start.22 = (bf16[208,768]{1,0:T(8,128)(2,1)S(1)}, bf16[208,768]{1,0:T(8,128)(2,1)S(1)}, u32[]{:S(2)}, u32[]{:S(2)}) collective-permute-start(bf16[208,768]{1,0:T(8,128)(2,1)S(1)} %get-tuple-element.68), channel_id=1, source_target_pairs={{0,32},{32,64},{64,96},{96,128},{128,160},{160,192},{192,224},{224... | collective-permute-start | bytes 958472 | tf_op jit(solution)/shard_map/ppermute | solution.py:380
  150.1 11.1 %collective-permute-start.31 = (bf16[192,768]{1,0:T(8,128)(2,1)S(1)}, bf16[192,768]{1,0:T(8,128)(2,1)S(1)}, u32[]{:S(2)}, u32[]{:S(2)}) collective-permute-start(bf16[192,768]{1,0:T(8,128)(2,1)S(1)} %get-tuple-element.75), channel_id=1, source_target_pairs={{0,32},{32,64},{64,96},{96,128},{128,160},{160,192},{192,224},{224... | collective-permute-start | bytes 884744 | tf_op jit(solution)/shard_map/ppermute | solution.py:380
  150.1 11.1 %collective-permute-start.24 = (bf16[208,768]{1,0:T(8,128)(2,1)S(1)}, bf16[208,768]{1,0:T(8,128)(2,1)S(1)}, u32[]{:S(2)}, u32[]{:S(2)}) collective-permute-start(bf16[208,768]{1,0:T(8,128)(2,1)S(1)} %get-tuple-element.69), channel_id=1, source_target_pairs={{0,224},{32,0},{64,32},{96,64},{128,96},{160,128},{192,160},{224,1... | collective-permute-start | bytes 958472 | tf_op jit(solution)/shard_map/ppermute | solution.py:380
  154.2 11.3 %collective-permute-start.23 = (bf16[208,768]{1,0:T(8,128)(2,1)S(1)}, bf16[208,768]{1,0:T(8,128)(2,1)S(1)}, u32[]{:S(2)}, u32[]{:S(2)}) collective-permute-start(bf16[208,768]{1,0:T(8,128)(2,1)S(1)} %backward.11), channel_id=1, source_target_pairs={{0,32},{32,64},{64,96},{96,128},{128,160},{160,192},{192,224},{224... | collective-permute-start | bytes 958472 | tf_op jit(solution)/shard_map/ppermute | solution.py:380
  155.7 9.6 %collective-permute-start.30 = (bf16[192,768]{1,0:T(8,128)(2,1)S(1)}, bf16[192,768]{1,0:T(8,128)(2,1)S(1)}, u32[]{:S(2)}, u32[]{:S(2)}) collective-permute-start(bf16[192,768]{1,0:T(8,128)(2,1)S(1)} %backward.15), channel_id=1, source_target_pairs={{0,224},{32,0},{64,32},{96,64},{128,96},{160,128},{192,160},{224,1... | collective-permute-start | bytes 884744 | tf_op jit(solution)/shard_map/ppermute | solution.py:380
  190.4 11.7 %collective-permute-start.32 = (bf16[144,768]{1,0:T(8,128)(2,1)S(1)}, bf16[144,768]{1,0:T(8,128)(2,1)S(1)}, u32[]{:S(2)}, u32[]{:S(2)}) collective-permute-start(bf16[144,768]{1,0:T(8,128)(2,1)S(1)} %combine.1.a_ref), channel_id=1, source_target_pairs={{0,1},{1,2},{2,3},{3,0},{4,5},{5,6},{6,7},{7,4},{8,9},{9,10},{10,1... | collective-permute-start | bytes 663560 | tf_op jit(solution)/shard_map/ppermute | solution.py:380
  (20 other events, 345.5 us)

commit v2 on v1

--- a/solution.py
+++ b/solution.py
@@ -407,7 +407,7 @@
 
     owns[0] = own
     hop(1, [])
-    hop(2, [owns[4]])
+    hop(2, [])
     hop(3, spread(0, 4))
     beside = spread(1, -1, 2, -2)
     low, high, *_ = lax.optimization_barrier(

time: 203 us -> 211 us (1.039)
  waiting for transfers between devices: 80.9 us -> 94.5 us
  starting transfers between devices: 49.4 us -> 41.9 us
    ppermute x35, waiting for transfers between devices: 80.9 us -> 94.5 us  [shift(): return lax.ppermute(a, axis, [(i, (i + by) % n) for i in range(n)])]
    ppermute x35, starting transfers between devices: 49.4 us -> 41.9 us  [shift(): return lax.ppermute(a, axis, [(i, (i + by) % n) for i in range(n)])]
  transfers between devices with their start and end apart: 35 -> 35, of which waited for: 21 -> 20; matrix products, arithmetic and copies ran while one was open for 0% -> 0% of each run, Pallas kernels for 9% -> 9%
where the time goes in v2:
time: 211 us; the launch traced here: 210 us
  waiting for transfers between devices  94.5 us (45%)
  starting transfers between devices  41.9 us (20%)
  blocking collectives  41 us (19%)
  Pallas kernels  27.3 us (13%)
  local copies, waits for them, and re-layouts  4.64 us (2%)
    ppermute x35, waiting for transfers between devices, shift(): return lax.ppermute(a, axis, [(i, (i + by) % n) for i in range(n)])  94.5 us
    ppermute x35, starting transfers between devices, shift(): return lax.ppermute(a, axis, [(i, (i + by) % n) for i in range(n)])  41.9 us
    all_to_all x1, blocking collectives, per_device(): rows = lax.all_to_all(rows, 'expert', split_axis=0, concat_axis=0)  21.5 us
    all_to_all x1, blocking collectives, per_device(): own = lax.all_to_all(own, 'expert', split_axis=0, concat_axis=0)  19.5 us
    pallas_call x8, Pallas kernels, backward(): pl.pallas_call(functools.partial(backward_kernel, ways, bool(received), f...  11.8 us
    pallas_call x2, Pallas kernels, forward(): pl.pallas_call(functools.partial(forward_kernel, count, split, len(after)...  10.3 us
    unnamed x18, local copies, waits for them, and re-layouts  4.44 us
  transfers between devices with their start and end apart: 35, of which 20 were waited for; matrix products, arithmetic and copies ran while one was open for 0% of the time, Pallas kernels for 9%

profile of v2, /device:TPU:1, one launch (start us, length us, event | category | flops | bytes accessed | tf_op | source)
XLA Modules:
  0.0 210.4 jit_solution(14933205259030561242)
XLA Ops:
  3.8 19.5 %all_to_all.10.refs_0_.refs_5_.refs_10_ = bf16[8,48,1152]{2,1,0:T(8,128)(2,1)S(1)} all-to-all(bf16[8,48,1152]{2,1,0:T(8,128)(2,1)S(1)} %dispatch.1), channel_id=1, replica_groups=mesh['dp'=8,'expert'=8,'tensor'=4] {'expert'}, dimensions={0} | all-to-all | bytes 1769472 | tf_op jit(solution)/shard_map/all_to_all | solution.py:389
  23.3 5.6 %collective-permute-start = (bf16[8,48,1152]{2,1,0:T(8,128)(2,1)S(1)}, bf16[8,48,1152]{2,1,0:T(8,128)(2,1)S(1)}, u32[]{:S(2)}, u32[]{:S(2)}) collective-permute-start(bf16[8,48,1152]{2,1,0:T(8,128)(2,1)S(1)} %all_to_all.10.refs_0_.refs_5_.refs_10_), channel_id=1, source_target_pairs={{0,224},{32,0},{64,32},{96,64},{128,96},{160,128},{192,160},{224,1... | collective-permute-start | bytes 2654216 | tf_op jit(solution)/shard_map/ppermute | solution.py:380
  28.9 18.1 %collective-permute-done.refs_1_.refs_6_.refs_11_ = bf16[8,48,1152]{2,1,0:T(8,128)(2,1)S(1)} collective-permute-done((bf16[8,48,1152]{2,1,0:T(8,128)(2,1)S(1)}, bf16[8,48,1152]{2,1,0:T(8,128)(2,1)S(1)}, u32[]{:S(2)}, u32[]{:S(2)}) %collective-permute-start) | collective-permute-done | bytes 884768 | tf_op jit(solution)/shard_map/ppermute | solution.py:380
  47.1 3.1 %collective-permute-done.1.refs_2_.refs_7_.refs_12_ = bf16[8,48,1152]{2,1,0:T(8,128)(2,1)S(1)} collective-permute-done((bf16[8,48,1152]{2,1,0:T(8,128)(2,1)S(1)}, bf16[8,48,1152]{2,1,0:T(8,128)(2,1)S(1)}, u32[]{:S(2)}, u32[]{:S(2)}) %collective-permute-start.1) | collective-permute-done | bytes 884768 | tf_op jit(solution)/shard_map/ppermute | solution.py:380
  53.3 20.3 %collective-permute-done.4.refs_10_ = bf16[8,48,128]{2,1,0:T(8,128)(2,1)S(1)} collective-permute-done((bf16[8,48,128]{2,1,0:T(8,128)(2,1)S(1)}, bf16[8,48,128]{2,1,0:T(8,128)(2,1)S(1)}, u32[]{:S(2)}, u32[]{:S(2)}) %collective-permute-start.4) | collective-permute-done | bytes 98336 | tf_op jit(solution)/shard_map/ppermute | solution.py:380
  73.6 2.8 %collective-permute-start.7 = (bf16[16,48,128]{2,1,0:T(8,128)(2,1)S(1)}, bf16[16,48,128]{2,1,0:T(8,128)(2,1)S(1)}, u32[]{:S(2)}, u32[]{:S(2)}) collective-permute-start(bf16[16,48,128]{2,1,0:T(8,128)(2,1)S(1)} %pad_maximum_fusion.1), channel_id=1, source_target_pairs={{0,2},{1,3},{2,0},{3,1},{4,6},{5,7},{6,4},{7,5},{8,10},{9,11},{10,... | collective-permute-start | bytes 589832 | tf_op jit(solution)/shard_map/ppermute | solution.py:380
  79.7 2.2 %collective-permute-done.6 = bf16[16,48,128]{2,1,0:T(8,128)(2,1)S(1)} collective-permute-done((bf16[16,48,128]{2,1,0:T(8,128)(2,1)S(1)}, bf16[16,48,128]{2,1,0:T(8,128)(2,1)S(1)}, u32[]{:S(2)}, u32[]{:S(2)}) %collective-permute-start.6) | collective-permute-done | bytes 196640 | tf_op jit(solution)/shard_map/ppermute | solution.py:380
  81.9 3.2 %collective-permute-done.5 = bf16[16,48,128]{2,1,0:T(8,128)(2,1)S(1)} collective-permute-done((bf16[16,48,128]{2,1,0:T(8,128)(2,1)S(1)}, bf16[16,48,128]{2,1,0:T(8,128)(2,1)S(1)}, u32[]{:S(2)}, u32[]{:S(2)}) %collective-permute-start.5) | collective-permute-done | bytes 196640 | tf_op jit(solution)/shard_map/ppermute | solution.py:380
  88.4 13.9 %collective-permute-done.11.refs_0_.refs_4_.refs_8_ = bf16[8,48,1152]{2,1,0:T(8,128)(2,1)S(1)} collective-permute-done((bf16[8,48,1152]{2,1,0:T(8,128)(2,1)S(1)}, bf16[8,48,1152]{2,1,0:T(8,128)(2,1)S(1)}, u32[]{:S(2)}, u32[]{:S(2)}) %collective-permute-start.11) | collective-permute-done | bytes 884768 | tf_op jit(solution)/shard_map/ppermute | solution.py:380
  103.7 2.3 %collective-permute-done.8 = bf16[32,48,128]{2,1,0:T(8,128)(2,1)S(1)} collective-permute-done((bf16[32,48,128]{2,1,0:T(8,128)(2,1)S(1)}, bf16[32,48,128]{2,1,0:T(8,128)(2,1)S(1)}, u32[]{:S(2)}, u32[]{:S(2)}) %collective-permute-start.8) | collective-permute-done | bytes 393248 | tf_op jit(solution)/shard_map/ppermute | solution.py:380
  112.4 5.6 %forward.2 = (bf16[48,512]{1,0:T(8,128)(2,1)S(1)}, f32[16,128]{1,0:T(8,128)S(1)}, bf16[48,512]{1,0:T(8,128)(2,1)S(1)}, f32[16,128]{1,0:T(8,128)S(1)}, bf16[48,51...) custom-call(s32[1]{0:T(128)} %bitcast.2.place_ref, ...), custom_call_target="tpu_custom_call" | custom-call | flops 2415919104 | bytes 9437184 | tf_op jit(solution)/shard_map/forward/pallas_call | solution.py:160
  118.1 4.8 %forward.3 = (bf16[48,512]{1,0:T(8,128)(2,1)S(1)}, f32[16,128]{1,0:T(8,128)S(1)}, bf16[48,512]{1,0:T(8,128)(2,1)S(1)}, f32[16,128]{1,0:T(8,128)S(1)}, bf16[48,51...) custom-call(s32[1]{0:T(128)} %bitcast.2.place_ref, bf16[8,48,1152]{2,1,0:T(8,128)(2,1)S(1)} %collective-permute-done.11.refs_0_.refs_4_.refs_8_, ...), custom_call_target="tpu_custom_call" | custom-call | flops 2415919104 | bytes 9437184 | tf_op jit(solution)/shard_map/forward/pallas_call | solution.py:160
  124.5 3.5 %collective-permute-start.19 = (bf16[208,768]{1,0:T(8,128)(2,1)S(1)}, bf16[208,768]{1,0:T(8,128)(2,1)S(1)}, u32[]{:S(2)}, u32[]{:S(2)}) collective-permute-start(bf16[208,768]{1,0:T(8,128)(2,1)S(1)} %get-tuple-element.65), channel_id=1, source_target_pairs={{0,224},{32,0},{64,32},{96,64},{128,96},{160,128},{192,160},{224,1... | collective-permute-start | bytes 958472 | tf_op jit(solution)/shard_map/ppermute | solution.py:380
  138.5 2.2 %collective-permute-done.26.refs_5_ = bf16[192,768]{1,0:T(8,128)(2,1)S(1)} collective-permute-done((bf16[192,768]{1,0:T(8,128)(2,1)S(1)}, bf16[192,768]{1,0:T(8,128)(2,1)S(1)}, u32[]{:S(2)}, u32[]{:S(2)}) %collective-permute-start.26) | collective-permute-done | bytes 294944 | tf_op jit(solution)/shard_map/ppermute | solution.py:380
  147.8 3.6 %collective-permute-done.27.refs_4_ = bf16[192,768]{1,0:T(8,128)(2,1)S(1)} collective-permute-done((bf16[192,768]{1,0:T(8,128)(2,1)S(1)}, bf16[192,768]{1,0:T(8,128)(2,1)S(1)}, u32[]{:S(2)}, u32[]{:S(2)}) %collective-permute-start.27) | collective-permute-done | bytes 294944 | tf_op jit(solution)/shard_map/ppermute | solution.py:380
  155.7 2.7 %collective-permute-start.24 = (bf16[208,768]{1,0:T(8,128)(2,1)S(1)}, bf16[208,768]{1,0:T(8,128)(2,1)S(1)}, u32[]{:S(2)}, u32[]{:S(2)}) collective-permute-start(bf16[208,768]{1,0:T(8,128)(2,1)S(1)} %get-tuple-element.69), channel_id=1, source_target_pairs={{0,224},{32,0},{64,32},{96,64},{128,96},{160,128},{192,160},{224,1... | collective-permute-start | bytes 958472 | tf_op jit(solution)/shard_map/ppermute | solution.py:380
  161.3 2.7 %collective-permute-start.30 = (bf16[192,768]{1,0:T(8,128)(2,1)S(1)}, bf16[192,768]{1,0:T(8,128)(2,1)S(1)}, u32[]{:S(2)}, u32[]{:S(2)}) collective-permute-start(bf16[192,768]{1,0:T(8,128)(2,1)S(1)} %backward.15), channel_id=1, source_target_pairs={{0,224},{32,0},{64,32},{96,64},{128,96},{160,128},{192,160},{224,1... | collective-permute-start | bytes 884744 | tf_op jit(solution)/shard_map/ppermute | solution.py:380
  164.0 2.8 %own_product.1.own_ref = f32[8,48,768]{2,1,0:T(8,128)S(1)} custom-call(bf16[48,512]{1,0:T(8,128)(2,1)S(1)} %get-tuple-element.44.g_ref, bf16[1,6144,256]{2,1,0:T(8,128)(2,1)S(1)} %copy-done, bf16[1,6144,256]{2,1,0:T(8,128)(2,1)S(1)} %copy-done.1), custom_call_target="tpu_custom_call" | custom-call | flops 805306368 | bytes 6291456 | tf_op jit(solution)/shard_map/own_product/pallas_call | solution.py:264
  166.8 4.0 %collective-permute-done.30.refs_2_ = bf16[192,768]{1,0:T(8,128)(2,1)S(1)} collective-permute-done((bf16[192,768]{1,0:T(8,128)(2,1)S(1)}, bf16[192,768]{1,0:T(8,128)(2,1)S(1)}, u32[]{:S(2)}, u32[]{:S(2)}) %collective-permute-start.30) | collective-permute-done | bytes 294944 | tf_op jit(solution)/shard_map/ppermute | solution.py:380
  171.3 21.5 %all_to_all.11.rows_ref = bf16[8,48,896]{2,1,0:T(8,128)(2,1)S(1)} all-to-all(bf16[8,48,896]{2,1,0:T(8,128)(2,1)S(1)} %last.1), channel_id=1, replica_groups=mesh['dp'=8,'expert'=8,'tensor'=4] {'expert'}, dimensions={0} | all-to-all | bytes 1376256 | tf_op jit(solution)/shard_map/all_to_all | solution.py:449
  193.6 2.5 %collective-permute-start.34 = (bf16[144,768]{1,0:T(8,128)(2,1)S(1)}, bf16[144,768]{1,0:T(8,128)(2,1)S(1)}, u32[]{:S(2)}, u32[]{:S(2)}) collective-permute-start(bf16[144,768]{1,0:T(8,128)(2,1)S(1)} %combine.1.a_ref), channel_id=1, source_target_pairs={{0,3},{1,0},{2,1},{3,2},{4,7},{5,4},{6,5},{7,6},{8,11},{9,8},{10,9... | collective-permute-start | bytes 663560 | tf_op jit(solution)/shard_map/ppermute | solution.py:380
  197.5 3.1 %collective-permute-done.34.d_ref = bf16[144,768]{1,0:T(8,128)(2,1)S(1)} collective-permute-done((bf16[144,768]{1,0:T(8,128)(2,1)S(1)}, bf16[144,768]{1,0:T(8,128)(2,1)S(1)}, u32[]{:S(2)}, u32[]{:S(2)}) %collective-permute-start.34) | collective-permute-done | bytes 221216 | tf_op jit(solution)/shard_map/ppermute | solution.py:380
  200.6 2.7 %collective-permute-done.33.c_ref = bf16[144,768]{1,0:T(8,128)(2,1)S(1)} collective-permute-done((bf16[144,768]{1,0:T(8,128)(2,1)S(1)}, bf16[144,768]{1,0:T(8,128)(2,1)S(1)}, u32[]{:S(2)}, u32[]{:S(2)}) %collective-permute-start.33) | collective-permute-done | bytes 221216 | tf_op jit(solution)/shard_map/ppermute | solution.py:380
  203.3 6.3 %collective-permute-done.32.b_ref = bf16[144,768]{1,0:T(8,128)(2,1)S(1)} collective-permute-done((bf16[144,768]{1,0:T(8,128)(2,1)S(1)}, bf16[144,768]{1,0:T(8,128)(2,1)S(1)}, u32[]{:S(2)}, u32[]{:S(2)}) %collective-permute-start.32) | collective-permute-done | bytes 221216 | tf_op jit(solution)/shard_map/ppermute | solution.py:380
  (93 shorter events, 50.4 us)
Async XLA Ops:
  23.3 23.7 %collective-permute-start = (bf16[8,48,1152]{2,1,0:T(8,128)(2,1)S(1)}, bf16[8,48,1152]{2,1,0:T(8,128)(2,1)S(1)}, u32[]{:S(2)}, u32[]{:S(2)}) collective-permute-start(bf16[8,48,1152]{2,1,0:T(8,128)(2,1)S(1)} %all_to_all.10.refs_0_.refs_5_.refs_10_), channel_id=1, source_target_pairs={{0,224},{32,0},{64,32},{96,64},{128,96},{160,128},{192,160},{224,1... | collective-permute-start | bytes 2654216 | tf_op jit(solution)/shard_map/ppermute | solution.py:380
  28.9 21.2 %collective-permute-start.1 = (bf16[8,48,1152]{2,1,0:T(8,128)(2,1)S(1)}, bf16[8,48,1152]{2,1,0:T(8,128)(2,1)S(1)}, u32[]{:S(2)}, u32[]{:S(2)}) collective-permute-start(bf16[8,48,1152]{2,1,0:T(8,128)(2,1)S(1)} %all_to_all.10.refs_0_.refs_5_.refs_10_), channel_id=1, source_target_pairs={{0,32},{32,64},{64,96},{96,128},{128,160},{160,192},{192,224},{224... | collective-permute-start | bytes 2654216 | tf_op jit(solution)/shard_map/ppermute | solution.py:380
  50.2 35.0 %collective-permute-start.2 = (bf16[8,48,1152]{2,1,0:T(8,128)(2,1)S(1)}, bf16[8,48,1152]{2,1,0:T(8,128)(2,1)S(1)}, u32[]{:S(2)}, u32[]{:S(2)}) collective-permute-start(bf16[8,48,1152]{2,1,0:T(8,128)(2,1)S(1)} %collective-permute-done.refs_1_.refs_6_.refs_11_), channel_id=1, source_target_pairs={{0,224},{32,0},{64,32},{96,64},{128,96},{160,128},{192,160},{224,1... | collective-permute-start | bytes 2654216 | tf_op jit(solution)/shard_map/ppermute | solution.py:380
  50.5 34.7 %collective-permute-start.3 = (bf16[8,48,1152]{2,1,0:T(8,128)(2,1)S(1)}, bf16[8,48,1152]{2,1,0:T(8,128)(2,1)S(1)}, u32[]{:S(2)}, u32[]{:S(2)}) collective-permute-start(bf16[8,48,1152]{2,1,0:T(8,128)(2,1)S(1)} %collective-permute-done.1.refs_2_.refs_7_.refs_12_), channel_id=1, source_target_pairs={{0,32},{32,64},{64,96},{96,128},{128,160},{160,192},{192,224},{224... | collective-permute-start | bytes 2654216 | tf_op jit(solution)/shard_map/ppermute | solution.py:380
  51.6 21.9 %collective-permute-start.4 = (bf16[8,48,128]{2,1,0:T(8,128)(2,1)S(1)}, bf16[8,48,128]{2,1,0:T(8,128)(2,1)S(1)}, u32[]{:S(2)}, u32[]{:S(2)}) collective-permute-start(bf16[8,48,128]{2,1,0:T(8,128)(2,1)S(1)} %slice.37), channel_id=1, source_target_pairs={{0,128},{32,160},{64,192},{96,224},{128,0},{160,32},{192,64},{224,... | collective-permute-start | bytes 294920 | tf_op jit(solution)/shard_map/ppermute | solution.py:380
  85.2 17.2 %collective-permute-start.11 = (bf16[8,48,1152]{2,1,0:T(8,128)(2,1)S(1)}, bf16[8,48,1152]{2,1,0:T(8,128)(2,1)S(1)}, u32[]{:S(2)}, u32[]{:S(2)}) collective-permute-start(bf16[8,48,1152]{2,1,0:T(8,128)(2,1)S(1)} %collective-permute-done.2.refs_3_.refs_8_.refs_13_), channel_id=1, source_target_pairs={{0,224},{32,0},{64,32},{96,64},{128,96},{160,128},{192,160},{224,1... | collective-permute-start | bytes 2654216 | tf_op jit(solution)/shard_map/ppermute | solution.py:380
  85.2 18.5 %collective-permute-start.12 = (bf16[8,48,1152]{2,1,0:T(8,128)(2,1)S(1)}, bf16[8,48,1152]{2,1,0:T(8,128)(2,1)S(1)}, u32[]{:S(2)}, u32[]{:S(2)}) collective-permute-start(bf16[8,48,1152]{2,1,0:T(8,128)(2,1)S(1)} %collective-permute-done.3.refs_4_.refs_9_.refs_14_), channel_id=1, source_target_pairs={{0,32},{32,64},{64,96},{96,128},{128,160},{160,192},{192,224},{224... | collective-permute-start | bytes 2654216 | tf_op jit(solution)/shard_map/ppermute | solution.py:380
  86.8 16.9 %collective-permute-start.10 = (bf16[32,48,128]{2,1,0:T(8,128)(2,1)S(1)}, bf16[32,48,128]{2,1,0:T(8,128)(2,1)S(1)}, u32[]{:S(2)}, u32[]{:S(2)}) collective-permute-start(bf16[32,48,128]{2,1,0:T(8,128)(2,1)S(1)} %pad_maximum_fusion), channel_id=1, source_target_pairs={{0,2},{1,3},{2,0},{3,1},{4,6},{5,7},{6,4},{7,5},{8,10},{9,11},{10,... | collective-permute-start | bytes 1179656 | tf_op jit(solution)/shard_map/ppermute | solution.py:380
  86.9 16.8 %collective-permute-start.9 = (bf16[32,48,128]{2,1,0:T(8,128)(2,1)S(1)}, bf16[32,48,128]{2,1,0:T(8,128)(2,1)S(1)}, u32[]{:S(2)}, u32[]{:S(2)}) collective-permute-start(bf16[32,48,128]{2,1,0:T(8,128)(2,1)S(1)} %pad_maximum_fusion), channel_id=1, source_target_pairs={{0,3},{1,0},{2,1},{3,2},{4,7},{5,4},{6,5},{7,6},{8,11},{9,8},{10,9... | collective-permute-start | bytes 1179656 | tf_op jit(solution)/shard_map/ppermute | solution.py:380
  87.3 18.7 %collective-permute-start.8 = (bf16[32,48,128]{2,1,0:T(8,128)(2,1)S(1)}, bf16[32,48,128]{2,1,0:T(8,128)(2,1)S(1)}, u32[]{:S(2)}, u32[]{:S(2)}) collective-permute-start(bf16[32,48,128]{2,1,0:T(8,128)(2,1)S(1)} %pad_maximum_fusion), channel_id=1, source_target_pairs={{0,1},{1,2},{2,3},{3,0},{4,5},{5,6},{6,7},{7,4},{8,9},{9,10},{10,1... | collective-permute-start | bytes 1179656 | tf_op jit(solution)/shard_map/ppermute | solution.py:380
  106.0 12.1 %collective-permute-start.13 = (bf16[4,48,1024]{2,1,0:T(8,128)(2,1)S(1)}, bf16[4,48,1024]{2,1,0:T(8,128)(2,1)S(1)}, u32[]{:S(2)}, u32[]{:S(2)}) collective-permute-start(bf16[4,48,1024]{2,1,0:T(8,128)(2,1)S(1)} %slice.42), channel_id=1, source_target_pairs={{0,32},{32,64},{64,96},{96,128},{128,160},{160,192},{192,224},{224... | collective-permute-start | bytes 1179656 | tf_op jit(solution)/shard_map/ppermute | solution.py:380
  106.5 11.6 %collective-permute-start.14 = (bf16[4,48,1024]{2,1,0:T(8,128)(2,1)S(1)}, bf16[4,48,1024]{2,1,0:T(8,128)(2,1)S(1)}, u32[]{:S(2)}, u32[]{:S(2)}) collective-permute-start(bf16[4,48,1024]{2,1,0:T(8,128)(2,1)S(1)} %slice.43), channel_id=1, source_target_pairs={{0,224},{32,0},{64,32},{96,64},{128,96},{160,128},{192,160},{224,1... | collective-permute-start | bytes 1179656 | tf_op jit(solution)/shard_map/ppermute | solution.py:380
  108.7 9.3 %collective-permute-start.17 = (bf16[16,48,128]{2,1,0:T(8,128)(2,1)S(1)}, bf16[16,48,128]{2,1,0:T(8,128)(2,1)S(1)}, u32[]{:S(2)}, u32[]{:S(2)}) collective-permute-start(bf16[16,48,128]{2,1,0:T(8,128)(2,1)S(1)} %pad_maximum_fusion.2), channel_id=1, source_target_pairs={{0,2},{1,3},{2,0},{3,1},{4,6},{5,7},{6,4},{7,5},{8,10},{9,11},{10,... | collective-permute-start | bytes 589832 | tf_op jit(solution)/shard_map/ppermute | solution.py:380
  131.0 9.7 %collective-permute-start.26 = (bf16[192,768]{1,0:T(8,128)(2,1)S(1)}, bf16[192,768]{1,0:T(8,128)(2,1)S(1)}, u32[]{:S(2)}, u32[]{:S(2)}) collective-permute-start(bf16[192,768]{1,0:T(8,128)(2,1)S(1)} %get-tuple-element.71), channel_id=1, source_target_pairs={{0,32},{32,64},{64,96},{96,128},{128,160},{160,192},{192,224},{224... | collective-permute-start | bytes 884744 | tf_op jit(solution)/shard_map/ppermute | solution.py:380
  133.8 11.9 %collective-permute-start.20 = (bf16[208,768]{1,0:T(8,128)(2,1)S(1)}, bf16[208,768]{1,0:T(8,128)(2,1)S(1)}, u32[]{:S(2)}, u32[]{:S(2)}) collective-permute-start(bf16[208,768]{1,0:T(8,128)(2,1)S(1)} %get-tuple-element.66), channel_id=1, source_target_pairs={{0,32},{32,64},{64,96},{96,128},{128,160},{160,192},{192,224},{224... | collective-permute-start | bytes 958472 | tf_op jit(solution)/shard_map/ppermute | solution.py:380
  135.2 10.5 %collective-permute-start.21 = (bf16[208,768]{1,0:T(8,128)(2,1)S(1)}, bf16[208,768]{1,0:T(8,128)(2,1)S(1)}, u32[]{:S(2)}, u32[]{:S(2)}) collective-permute-start(bf16[208,768]{1,0:T(8,128)(2,1)S(1)} %get-tuple-element.67), channel_id=1, source_target_pairs={{0,224},{32,0},{64,32},{96,64},{128,96},{160,128},{192,160},{224,1... | collective-permute-start | bytes 958472 | tf_op jit(solution)/shard_map/ppermute | solution.py:380
  142.2 9.1 %collective-permute-start.27 = (bf16[192,768]{1,0:T(8,128)(2,1)S(1)}, bf16[192,768]{1,0:T(8,128)(2,1)S(1)}, u32[]{:S(2)}, u32[]{:S(2)}) collective-permute-start(bf16[192,768]{1,0:T(8,128)(2,1)S(1)} %get-tuple-element.72), channel_id=1, source_target_pairs={{0,224},{32,0},{64,32},{96,64},{128,96},{160,128},{192,160},{224,1... | collective-permute-start | bytes 884744 | tf_op jit(solution)/shard_map/ppermute | solution.py:380
  143.1 9.3 %collective-permute-start.28 = (bf16[192,768]{1,0:T(8,128)(2,1)S(1)}, bf16[192,768]{1,0:T(8,128)(2,1)S(1)}, u32[]{:S(2)}, u32[]{:S(2)}) collective-permute-start(bf16[192,768]{1,0:T(8,128)(2,1)S(1)} %get-tuple-element.73), channel_id=1, source_target_pairs={{0,32},{32,64},{64,96},{96,128},{128,160},{160,192},{192,224},{224... | collective-permute-start | bytes 884744 | tf_op jit(solution)/shard_map/ppermute | solution.py:380
  147.2 11.1 %collective-permute-start.22 = (bf16[208,768]{1,0:T(8,128)(2,1)S(1)}, bf16[208,768]{1,0:T(8,128)(2,1)S(1)}, u32[]{:S(2)}, u32[]{:S(2)}) collective-permute-start(bf16[208,768]{1,0:T(8,128)(2,1)S(1)} %get-tuple-element.68), channel_id=1, source_target_pairs={{0,32},{32,64},{64,96},{96,128},{128,160},{160,192},{192,224},{224... | collective-permute-start | bytes 958472 | tf_op jit(solution)/shard_map/ppermute | solution.py:380
  155.7 11.1 %collective-permute-start.31 = (bf16[192,768]{1,0:T(8,128)(2,1)S(1)}, bf16[192,768]{1,0:T(8,128)(2,1)S(1)}, u32[]{:S(2)}, u32[]{:S(2)}) collective-permute-start(bf16[192,768]{1,0:T(8,128)(2,1)S(1)} %get-tuple-element.75), channel_id=1, source_target_pairs={{0,32},{32,64},{64,96},{96,128},{128,160},{160,192},{192,224},{224... | collective-permute-start | bytes 884744 | tf_op jit(solution)/shard_map/ppermute | solution.py:380
  155.7 11.1 %collective-permute-start.24 = (bf16[208,768]{1,0:T(8,128)(2,1)S(1)}, bf16[208,768]{1,0:T(8,128)(2,1)S(1)}, u32[]{:S(2)}, u32[]{:S(2)}) collective-permute-start(bf16[208,768]{1,0:T(8,128)(2,1)S(1)} %get-tuple-element.69), channel_id=1, source_target_pairs={{0,224},{32,0},{64,32},{96,64},{128,96},{160,128},{192,160},{224,1... | collective-permute-start | bytes 958472 | tf_op jit(solution)/shard_map/ppermute | solution.py:380
  159.8 11.3 %collective-permute-start.23 = (bf16[208,768]{1,0:T(8,128)(2,1)S(1)}, bf16[208,768]{1,0:T(8,128)(2,1)S(1)}, u32[]{:S(2)}, u32[]{:S(2)}) collective-permute-start(bf16[208,768]{1,0:T(8,128)(2,1)S(1)} %backward.11), channel_id=1, source_target_pairs={{0,32},{32,64},{64,96},{96,128},{128,160},{160,192},{192,224},{224... | collective-permute-start | bytes 958472 | tf_op jit(solution)/shard_map/ppermute | solution.py:380
  161.3 9.5 %collective-permute-start.30 = (bf16[192,768]{1,0:T(8,128)(2,1)S(1)}, bf16[192,768]{1,0:T(8,128)(2,1)S(1)}, u32[]{:S(2)}, u32[]{:S(2)}) collective-permute-start(bf16[192,768]{1,0:T(8,128)(2,1)S(1)} %backward.15), channel_id=1, source_target_pairs={{0,224},{32,0},{64,32},{96,64},{128,96},{160,128},{192,160},{224,1... | collective-permute-start | bytes 884744 | tf_op jit(solution)/shard_map/ppermute | solution.py:380
  196.7 12.9 %collective-permute-start.32 = (bf16[144,768]{1,0:T(8,128)(2,1)S(1)}, bf16[144,768]{1,0:T(8,128)(2,1)S(1)}, u32[]{:S(2)}, u32[]{:S(2)}) collective-permute-start(bf16[144,768]{1,0:T(8,128)(2,1)S(1)} %combine.1.a_ref), channel_id=1, source_target_pairs={{0,1},{1,2},{2,3},{3,0},{4,5},{5,6},{6,7},{7,4},{8,9},{9,10},{10,1... | collective-permute-start | bytes 663560 | tf_op jit(solution)/shard_map/ppermute | solution.py:380
  (20 other events, 357.1 us)
